TPU v7x, 32 devices: a whole 2x2x4 slice. The times are simulated.
32 devices in a mesh: gene: 4 (over y, x), sample: 2 (over core), variant: 4 (over z).
Axes of the slice: x: 2, y: 2, z: 4, core: 2. Of those that a mesh axis runs over, the one named last changes fastest.
Arguments:
- expression: bfloat16 [8192, 4096], P('sample', 'gene'), may hold values from -6 to 6
- profile: float32 [4096, 7], P('gene'), may hold values from -0.25 to 0.25
- dosage: int32 [8192, 512], P('sample', 'variant'), may hold values from 0 to 2
- signature: int32 [500], replicated, may hold values from 0 to 4095, as said below
Outputs:
- interaction: float32 [3584, 4096], P(('variant', 'sample'), 'gene')
- proportions: float32 [8192, 7], P('sample')
Inputs may be any that keep to these rules, and one draw needn't show every extreme that they name: `signature`: distinct gene indices; gene 0 and gene 4096 - 1 are always among them.
All inputs are finite; a program needn't handle non-finite values.
Results may differ from a plain program's by a relative error of at most 0.0045.
Values sent between devices are 32-bit elements; how exact they have to be, the bound alone decides.
No kernel may reach another device: no remote copies, remote signals or barrier semaphores. Data moves between devices by JAX's collectives and lax.ppermute only.
A program may use at most 128 MiB of HBM per device.

v0:
```python
import math

import jax
import jax.numpy as jnp
from jax import lax
from jax.sharding import PartitionSpec as P


def chol_solve(gram, rhs):
    factor = jnp.linalg.cholesky(gram)
    return jax.scipy.linalg.cho_solve((factor, True), rhs)


def local(expression, profile, dosage, signature):
    high = lax.Precision.HIGHEST
    s_dev, g_dev = expression.shape
    v_dev = dosage.shape[1]
    types = profile.shape[1]
    offset = lax.axis_index("gene") * g_dev
    local_ids = offset + lax.iota(jnp.int32, g_dev)
    member = jnp.any(local_ids[:, None] == signature[None, :], axis=1).astype(jnp.float32)
    masked = profile * member[:, None]
    gram = jnp.dot(masked.T, masked, precision=high)
    rhs = jnp.dot(masked.T, expression.T, precision=high, preferred_element_type=jnp.float32)
    gram_all = lax.psum(gram, "gene")
    rhs_share = lax.psum_scatter(rhs, "gene", scatter_dimension=1, tiled=True)
    share_t = chol_solve(gram_all, rhs_share)
    props_t = lax.all_gather(share_t, "gene", axis=1, tiled=True)
    props = props_t.T
    pp_mat = jnp.dot(props_t, props, precision=high)
    py_mat = jnp.dot(props_t, expression, precision=high, preferred_element_type=jnp.float32)
    rounded = props.astype(jnp.bfloat16)
    design = (dosage.astype(jnp.bfloat16)[:, :, None] * rounded[:, None, :]).reshape(
        s_dev, v_dev * types
    )
    weights = (rounded.astype(jnp.float32)[:, :, None] * props[:, None, :]).reshape(
        s_dev, types * types
    )
    corr_t = jnp.dot(weights.T, dosage.astype(jnp.float32), precision=high)
    corr_t = corr_t.reshape(types, types, v_dev).transpose(1, 2, 0).reshape(types, v_dev * types)
    pp_all, py_all = lax.psum((pp_mat, py_mat), "sample")
    coef = chol_solve(pp_all, py_all)
    n_sample = lax.axis_size("sample")
    scale = jnp.float32(1.0 / math.sqrt(s_dev * n_sample))
    cross = lax.psum_scatter(
        lax.dot_general(
            design, expression, (((0,), (0,)), ((), ())), preferred_element_type=jnp.float32
        ),
        "sample",
        scatter_dimension=0,
        tiled=True,
    )
    corr_share = lax.psum_scatter(corr_t, "sample", scatter_dimension=1, tiled=True)
    interaction = (cross - jnp.dot(corr_share.T, coef, precision=high)) * scale
    return (interaction, props)


def solution(mesh):
    placed = (P("sample", "gene"), P("gene", None), P("sample", "variant"), P())
    return jax.shard_map(
        local,
        mesh=mesh,
        in_specs=placed,
        out_specs=(P(("variant", "sample"), "gene"), P("sample", None)),
        check_vma=False,
    )
```

profile of v0, /device:TPU:0, one launch (start us, length us, event | category | flops | bytes accessed | tf_op | source)
XLA Modules:
  0.0 112.6 jit_solution(16239084680992510847)
XLA Ops:
  7.2 1.2 %compare_reduce_fusion = pred[1024]{0:T(1024)(128)(4,1)S(1)} fusion(s32[1024]{0:T(1024)S(1)} %iota_add_fusion, s32[500]{0:T(512)} %param.10), kind=kLoop, calls=%fused_computation.4 | loop fusion | flops 1022976 | bytes 7120 | tf_op jit(solution)/shard_map/reduce_or | solution.py:21
  8.4 10.7 %fusion.7 = f32[7,4096]{1,0:T(8,128)} fusion(bf16[4096,1024]{1,0:T(8,128)(2,1)} %param.7, f32[1024,7]{0,1:T(8,128)} %param.8, f32[1024]{0:T(1024)S(1)} %convert_element_type.20), kind=kOutput, calls=%fused_computation.9 | convolution fusion | flops 352328704 | bytes 8536064 | tf_op jit(solution)/shard_map/dot_general | solution.py:24
  19.3 11.4 %psum.21 = f32[7,7]{0,1:T(8,128)S(1)} all-reduce(f32[7,7]{0,1:T(8,128)S(1)} %fusion.9), channel_id=1, replica_groups=mesh['gene'=4,'sample'=2,'variant'=4] {'gene'}, use_global_device_ids=true, to_apply=%region_1.0 | all-reduce | flops 49 | bytes 392 | tf_op jit(solution)/shard_map/psum | solution.py:25
  30.8 0.6 cholesky.44
  31.4 0.6 compare_reduce_fusion.2
  32.1 0.6 fusion.13
  32.7 0.5 custom-call.8
  33.3 1.1 convert_element_type.19
  34.4 1.5 %copy.29 = bf16[4096,128]{0,1:T(8,128)(2,1)S(1)} copy(bf16[4096,128]{1,0:T(8,128)(2,1)} %convert_element_type.19) | data formatting | bytes 2097152 | tf_op jit(solution)/shard_map/convert_element_type | solution.py:33
  35.9 10.0 %reduce-scatter.6.cloned.1.call-done = f32[7,1024]{1,0:T(8,128)} async-done(((f32[7,4096]{1,0:T(8,128)}), f32[7,1024]{1,0:T(8,128)}) %reduce-scatter.6.cloned.1.call-update) | async-done | bytes 28688 | tf_op jit(solution)/shard_map/reduce_scatter | solution.py:26
  45.8 1.0 fusion.19
  46.8 0.2 fusion.21
  47.0 8.6 %all_gather.3 = f32[7,4096]{1,0:T(8,128)S(1)} all-gather(f32[7,1024]{1,0:T(8,128)S(1)} %fusion.21), channel_id=1, replica_groups=mesh['gene'=4,'sample'=2,'variant'=4] {'gene'}, dimensions={1}, use_global_device_ids=true | all-gather | bytes 143360 | tf_op jit(solution)/shard_map/all_gather | solution.py:28
  55.6 4.3 %broadcast_multiply_fusion = bf16[4096,128,7]{0,2,1:T(8,128)(2,1)} fusion(bf16[4096,7]{0,1:T(8,128)(2,1)S(1)} %get-tuple-element.7, bf16[4096,128]{0,1:T(8,128)(2,1)S(1)} %copy.29), kind=kLoop, calls=%fused_computation | loop fusion | flops 3670016 | bytes 8445952 | tf_op jit(solution)/shard_map/mul | solution.py:33
  59.9 9.5 %mul.57 = bf16[4096,896]{0,1:T(8,128)(2,1)} reshape(bf16[4096,128,7]{0,2,1:T(8,128)(2,1)} %broadcast_multiply_fusion) | data formatting | bytes 14680064 | tf_op jit(solution)/shard_map/mul | solution.py:33
  69.4 1.0 mul.61
  70.5 1.3 %dot_general.29 = f32[7,7,4096]{2,1,0:T(8,128)S(1)} reshape(f32[49,4096]{1,0:T(8,128)} %bitcast.61) | data formatting | bytes 1605632 | tf_op jit(solution)/shard_map/dot_general | solution.py:39
  71.8 1.7 %fusion.3 = f32[7,128,7]{1,0,2:T(8,128)S(1)} fusion(f32[7,7,4096]{2,1,0:T(8,128)S(1)} %dot_general.29, s32[4096,128]{1,0:T(8,128)S(1)} %copy-done), kind=kOutput, calls=%fused_computation.6 | convolution fusion | flops 308805632 | bytes 2925056 | tf_op jit(solution)/shard_map/dot_general | solution.py:39
  73.4 0.3 copy.41
  73.7 0.8 reshape.43
  74.6 0.2 reduce-scatter.8.cloned.1.call-start
  74.8 13.5 %fusion.26 = f32[896,1024]{1,0:T(8,128)} fusion(bf16[4096,896]{0,1:T(8,128)(2,1)} %mul.57, bf16[4096,1024]{1,0:T(8,128)(2,1)} %param.7), kind=kOutput, calls=%fused_computation.39 | convolution fusion | flops 7516192768 | bytes 19398656 | tf_op jit(solution)/shard_map/dot_general | solution.py:46
  88.4 0.3 fusion.27
  88.7 5.7 %fusion.28 = f32[7,1024]{1,0:T(8,128)S(1)} fusion(f32[7,4096]{1,0:T(8,128)S(1)} %all_gather.3, bf16[4096,1024]{1,0:T(8,128)(2,1)} %param.7), kind=kOutput, calls=%fused_computation.41 | convolution fusion | flops 352321536 | bytes 8531968 | tf_op jit(solution)/shard_map/dot_general | solution.py:31
  94.4 3.5 %all-reduce = (f32[7,1024]{1,0:T(8,128)S(1)}, f32[7,7]{0,1:T(8,128)S(1)}) all-reduce(f32[7,1024]{1,0:T(8,128)S(1)} %fusion.28, f32[7,7]{0,1:T(8,128)S(1)} %fusion.27), channel_id=1, replica_groups=mesh['gene'=4,'sample'=2,'variant'=4] {'sample'}, use_global_device_ids=true, to_apply=%region_8.11 | all-reduce | flops 7217 | bytes 57736 | tf_op jit(solution)/shard_map/psum | solution.py:41
  98.0 0.6 cholesky.55
  98.7 0.6 compare_reduce_fusion.1
  99.3 0.7 fusion.14
  100.0 0.5 custom-call.9
  100.5 0.2 fusion.15
  101.0 4.5 %subtract_multiply_fusion = f32[448,1024]{1,0:T(8,128)} fusion(f32[448,1024]{1,0:T(8,128)} %reduce-scatter.8.cloned.1.call-done, f32[7,1024]{1,0:T(8,128)S(1)} %fusion.17, f32[448,7]{1,0:T(8,128)} %reduce-scatter.10.cloned.1.call-done), kind=kOutput, calls=%fused_computation.5 | convolution fusion | flops 39452672 | bytes 3711232 | tf_op jit(solution)/shard_map/dot_general | solution.py:54
  105.5 0.7 copy.44
  (23 shorter events, 0.9 us)
Async XLA Ops:
  7.2 12.0 %copy-start.1 = (f32[1024,7]{0,1:T(8,128)S(1)}, f32[1024,7]{0,1:T(8,128)}, u32[]{:S(2)}) copy-start(f32[1024,7]{0,1:T(8,128)} %param.8) | copy-start | bytes 86020
  7.2 26.1 %copy-start = (s32[4096,128]{1,0:T(8,128)S(1)}, s32[4096,128]{1,0:T(8,128)}, u32[]{:S(2)}) copy-start(s32[4096,128]{1,0:T(8,128)} %param.9) | copy-start | bytes 6291460
  7.2 38.7 %reduce-scatter.6.cloned.1.call-start = ((), (), s32[]{:S(2)}) async-start(), calls=%async_computation.3 | async-start | bytes 163840 | tf_op jit(solution)/shard_map/reduce_scatter | solution.py:26
  19.1 81.8 %reduce-scatter.10.cloned.1.call-start = ((), (), s32[]{:S(2)}) async-start(), calls=%async_computation.5 | async-start | bytes 688128
  74.6 26.4 %reduce-scatter.8.cloned.1.call-start = ((), (), s32[]{:S(2)}) async-start(), calls=%async_computation.4 | async-start | bytes 5505024 | tf_op jit(solution)/shard_map/reduce_scatter | solution.py:45
Sparse Core Ops, SparseCore 0:
  19.2 26.5 reduce-scatter.5
  74.7 7.8 reduce-scatter.9
  88.5 11.5 reduce-scatter.7
where the time goes:
time: 113 us
  matrix products  38.1 us (34%)
  blocking collectives  23.4 us (21%)
  local copies, waits for them, and re-layouts  15.2 us (13%)
  between operations  13.9 us (12%)
  other arithmetic  11.6 us (10%)
  waiting for transfers between devices  10.1 us (9%)
    dot_general x1, matrix products, local(): lax.dot_general(design, expression, (((0,), (0,)), ((), ())), preferred_e...  13.5 us
    psum x1, blocking collectives, local(): gram_all = lax.psum(gram, 'gene')  11.4 us
    dot_general x1, matrix products, local(): jnp.dot(masked.T, expression.T, precision=high, preferred_element_type=jn...  10.7 us
    reduce_scatter x1, waiting for transfers between devices, local(): rhs_share = lax.psum_scatter(rhs, 'gene', scatter_dimension=1, tiled=True)  9.99 us
    mul x1, local copies, waits for them, and re-layouts, local(): dosage.astype(jnp.bfloat16)[:, :, None] * rounded[:, None, :]  9.5 us
    all_gather x1, blocking collectives, local(): props_t = lax.all_gather(share_t, 'gene', axis=1, tiled=True)  8.57 us
    dot_general x1, matrix products, local(): jnp.dot(props_t, expression, precision=high, preferred_element_type=jnp.f...  5.69 us
    dot_general x1, matrix products, local(): interaction = (cross - jnp.dot(corr_share.T, coef, precision=high)) * scale  4.49 us
  transfers between devices with their start and end apart: 3, of which 1 were waited for; matrix products, arithmetic and copies ran while one was open for 25% of the time, Pallas kernels for 0%

commit v1 on v0

v1 whole, which is shorter than its diff:
```python
import functools
import math

import jax
import jax.numpy as jnp
from jax import lax
from jax.experimental import pallas as pl
from jax.experimental.pallas import tpu as pltpu
from jax.sharding import PartitionSpec as P

F32 = jnp.float32
BF16 = jnp.bfloat16
VMEM_LIMIT = 32 << 20
LANES = 128
ROWS = 8


def round_up(n, m):
    return (n + m - 1) // m * m


def in_hbm(x):
    return pltpu.with_memory_space_constraint(x, pltpu.HBM)


def split3(x):
    hi = x.astype(BF16).astype(F32)
    rest = x - hi
    mid = rest.astype(BF16).astype(F32)
    return hi, mid, rest - mid


def stacked(parts, rows):
    have = sum(p.shape[0] for p in parts)
    if have < rows:
        parts = list(parts) + [jnp.zeros((rows - have, parts[0].shape[1]), F32)]
    return jnp.concatenate(parts, axis=0).astype(BF16)


def put(index_row, index_col, values, shape):
    row = lax.broadcasted_iota(jnp.int32, shape, 0)
    col = lax.broadcasted_iota(jnp.int32, shape, 1)
    out = jnp.zeros(shape, F32)
    for (i, j), value in values.items():
        hit = (col == j) if i is None else ((row == i) & (col == j))
        out = jnp.where(hit, value, out)
    return out


def cholesky(entry, n):
    low = {}
    inv = []
    for j in range(n):
        d = entry(j, j)
        for k in range(j):
            d = d - low[j, k] * low[j, k]
        root = jnp.sqrt(d)
        low[j, j] = root
        inv.append(1.0 / root)
        for i in range(j + 1, n):
            v = entry(i, j)
            for k in range(j):
                v = v - low[i, k] * low[j, k]
            low[i, j] = v * inv[j]
    return low, inv


def substitute(low, inv, right):
    n = len(right)
    y = []
    for i in range(n):
        v = right[i]
        for k in range(i):
            v = v - low[i, k] * y[k]
        y.append(v * inv[i])
    x = [None] * n
    for i in reversed(range(n)):
        v = y[i]
        for k in range(i + 1, n):
            v = v - low[k, i] * x[k]
        x[i] = v * inv[i]
    return x


def entries(tile):
    cache = {}

    def entry(i, j):
        if (i, j) not in cache:
            cache[i, j] = jnp.broadcast_to(tile[i : i + 1, j : j + 1], (ROWS, LANES))
        return cache[i, j]

    return entry


def wide(tile, like):
    rows, cols = like
    if rows == 1:
        return jnp.concatenate([tile[0:1]] * (cols // LANES), axis=1)
    return jnp.concatenate([tile] * (rows // ROWS), axis=0)


def rhs_kernel(
    types, pieces, signature_in, profile_in, expression, held, parts, signature, profile, sems, few
):
    samples, genes = expression.shape
    step = samples // pieces
    copies = []
    early = [
        pltpu.make_async_copy(signature_in, signature, few.at[0]),
        pltpu.make_async_copy(profile_in, profile, few.at[1]),
    ]
    for copy in early:
        copy.start()
    for i in range(pieces):
        rows = pl.ds(i * step, step)
        copy = pltpu.make_async_copy(expression.at[rows], held.at[rows], sems.at[i])
        copy.start()
        copies.append(copy)

    for copy in early:
        copy.wait()
    groups = genes // LANES
    base = lax.axis_index("gene") * genes
    shape = (groups, LANES)
    ids = (
        base
        + lax.broadcasted_iota(jnp.int32, shape, 0) * LANES
        + lax.broadcasted_iota(jnp.int32, shape, 1)
    )

    n_sig = signature.shape[0]
    unroll = 10 if n_sig % 10 == 0 else 1

    def look(i, member):
        for u in range(unroll):
            member = member | (ids == signature[i * unroll + u]).astype(jnp.int32)
        return member

    member = lax.fori_loop(0, n_sig // unroll, look, jnp.zeros(shape, jnp.int32))
    member = (member > 0).astype(F32)
    row = jnp.concatenate([member[h : h + 1] for h in range(groups)], axis=1)
    masked = profile[...] * row
    masked = jnp.concatenate([masked, jnp.zeros((ROWS - types, genes), F32)], axis=0)
    left = stacked(split3(masked), 32)

    gram = {}
    for j in range(types):
        gram[None, j] = jnp.sum(masked * masked[j : j + 1], axis=1, keepdims=True)
    parts[types * samples // LANES :, :] = put(None, None, gram, (ROWS, LANES))

    for i in range(pieces):
        copies[i].wait()
        out = lax.dot_general(
            left,
            held[i * step : (i + 1) * step, :],
            (((1,), (1,)), ((), ())),
            preferred_element_type=F32,
        )
        out = out[0:ROWS] + (out[ROWS : 2 * ROWS] + out[2 * ROWS : 3 * ROWS])
        for c in range(step // LANES):
            at = (i * step // LANES + c) * types
            parts[at : at + types, :] = out[:types, c * LANES : (c + 1) * LANES]


def right_sides(expression, profile_t, signature):
    samples, genes = expression.shape
    types = profile_t.shape[0]
    pieces = 8
    rows = types * samples // LANES + ROWS
    return pl.pallas_call(
        functools.partial(rhs_kernel, types, pieces),
        in_specs=[pl.BlockSpec(memory_space=pltpu.HBM)] * 3,
        out_specs=[pl.BlockSpec(memory_space=pltpu.VMEM)] * 2,
        out_shape=[
            pltpu.VMEM((samples, genes), BF16),
            jax.ShapeDtypeStruct((rows, LANES), F32),
        ],
        scratch_shapes=[
            pltpu.SMEM(signature.shape, jnp.int32),
            pltpu.VMEM(profile_t.shape, F32),
            pltpu.SemaphoreType.DMA((pieces,)),
            pltpu.SemaphoreType.DMA((2,)),
        ],
        compiler_params=pltpu.CompilerParams(vmem_limit_bytes=VMEM_LIMIT),
        cost_estimate=pl.CostEstimate(
            flops=2 * 32 * samples * genes, bytes_accessed=2 * samples * genes, transcendentals=0
        ),
        name="right_sides",
    )(in_hbm(signature), in_hbm(profile_t), in_hbm(expression))


def dosage_kernel(own, dosage, first, rest):
    block, variants = dosage.shape
    wide_d = dosage[...].astype(F32)
    if own < variants:
        place = lax.axis_index("sample") * own
        wide_d = pltpu.roll(wide_d, lax.rem(variants - place, variants), 1)
    turned = wide_d.T
    pad = first.shape[0] - own
    mine = turned[:own]
    if pad:
        mine = jnp.concatenate([mine, jnp.zeros((pad, block), F32)], axis=0)
    first[...] = mine.astype(BF16)
    left = variants - own
    if left:
        others = turned[own:]
        pad = rest.shape[0] - left
        if pad:
            others = jnp.concatenate([others, jnp.zeros((pad, block), F32)], axis=0)
        rest[...] = others.astype(BF16)


def turn_dosage(dosage, own):
    samples, variants = dosage.shape
    block = 512
    first, rest = round_up(own, 16), round_up(variants - own, 16)
    return pl.pallas_call(
        functools.partial(dosage_kernel, own),
        grid=(samples // block,),
        in_specs=[pl.BlockSpec((block, variants), lambda i: (i, 0))],
        out_specs=[
            pl.BlockSpec((first, block), lambda i: (0, i)),
            pl.BlockSpec((rest, block), lambda i: (0, i)),
        ],
        out_shape=[
            jax.ShapeDtypeStruct((first, samples), BF16),
            jax.ShapeDtypeStruct((rest, samples), BF16),
        ],
        compiler_params=pltpu.CompilerParams(vmem_limit_bytes=VMEM_LIMIT),
        cost_estimate=pl.CostEstimate(
            flops=samples * variants, bytes_accessed=6 * samples * variants, transcendentals=0
        ),
        name="turn_dosage",
    )(in_hbm(dosage))


def design_rows(left, dosage, rounded, cols, count):
    types = len(rounded)
    width = rounded[0].shape[1]
    for k in range(types):
        spread = jnp.broadcast_to(rounded[k], (16, width)).astype(BF16)
        for q in range(count // 16):
            at = k * count + q * 16
            left[at : at + 16, :] = dosage[q * 16 : q * 16 + 16, cols] * spread


def first_kernel(
    types, step, own_parts, *refs
):
    (x_parts, y_parts, d_parts, mine, others, held, cross, props, kept, small, corr_own, corr_oth, left, weights, packed) = refs
    samples, genes = held.shape
    groups = samples // LANES
    last = types * groups
    n_mine, n_others = mine.shape[0], others.shape[0]

    def total(rows):
        return (own_parts[rows, :] + x_parts[rows, :]) + (y_parts[rows, :] + d_parts[rows, :])

    gram = total(slice(last, last + ROWS))
    low, inv = cholesky(entries(gram), types)
    like = (groups, LANES)
    low = {key: wide(value, like) for key, value in low.items() if key[0] != key[1]}
    inv = [wide(value, like) for value in inv]
    right = [total(pl.ds(k, groups, stride=types)) for k in range(types)]
    solved = substitute(low, inv, right)

    pp = {}
    for i in range(types):
        for j in range(i, types):
            value = jnp.sum(solved[i] * solved[j], axis=(0, 1), keepdims=True)
            pp[i, j] = value
            pp[j, i] = value
    small[ROWS:, :] = jnp.concatenate(
        [put(None, None, pp, (ROWS, LANES)), jnp.zeros((ROWS, genes - LANES), F32)], axis=1
    )

    for k in range(types):
        packed[pl.ds(k, groups, stride=ROWS), :] = solved[k]
    packed[pl.ds(types, groups, stride=ROWS), :] = jnp.zeros(like, F32)

    n_rows = types * n_others
    for c in range(samples // step):
        cols = slice(c * step, (c + 1) * step)
        at = c * step // LANES * ROWS
        p = jnp.concatenate(
            [packed[at + g * ROWS : at + (g + 1) * ROWS, :] for g in range(step // LANES)], axis=1
        )
        props[:, cols] = p[:types]
        pieces = split3(p)
        kept[:, cols] = pieces[0]
        rounded = [pieces[0][k : k + 1] for k in range(types)]
        design_rows(left, others, rounded, cols, n_others)
        left[n_rows:, :] = stacked(pieces, 32)
        w = jnp.concatenate([r * p for r in rounded], axis=0)
        w_parts = split3(w)
        span = ROWS * types
        for s in range(3):
            weights[s * 64 : s * 64 + 64, :] = stacked([w_parts[s]], 64)
        out = jnp.dot(left[...], held[cols, :], preferred_element_type=F32)
        contract = (((1,), (1,)), ((), ()))
        co = lax.dot_general(others[:, cols], weights[...], contract, preferred_element_type=F32)
        cm = lax.dot_general(mine[:, cols], weights[...], contract, preferred_element_type=F32)
        extra = out[n_rows : n_rows + ROWS] + (
            out[n_rows + ROWS : n_rows + 2 * ROWS] + out[n_rows + 2 * ROWS : n_rows + 3 * ROWS]
        )
        if c == 0:
            cross[...] = out[:n_rows]
            small[:ROWS, :] = extra
            corr_oth[...] = co
            corr_own[...] = cm
        else:
            cross[...] += out[:n_rows]
            small[:ROWS, :] += extra
            corr_oth[...] += co
            corr_own[...] += cm


def first_products(parts, mine, others, held, types):
    samples, genes = held.shape
    step = 512
    n_mine, n_others = mine.shape[0], others.shape[0]
    vmem = pl.BlockSpec(memory_space=pltpu.VMEM)
    return pl.pallas_call(
        functools.partial(first_kernel, types, step),
        in_specs=[vmem] * 7,
        out_specs=[vmem] * 6,
        out_shape=[
            jax.ShapeDtypeStruct((types * n_others, genes), F32),
            jax.ShapeDtypeStruct((types, samples), F32),
            pltpu.VMEM((ROWS, samples), F32),
            jax.ShapeDtypeStruct((2 * ROWS, genes), F32),
            jax.ShapeDtypeStruct((n_mine, 192), F32),
            jax.ShapeDtypeStruct((n_others, 192), F32),
        ],
        scratch_shapes=[
            pltpu.VMEM((types * n_others + 32, step), BF16),
            pltpu.VMEM((192, step), BF16),
            pltpu.VMEM((samples // LANES * ROWS, LANES), F32),
        ],
        compiler_params=pltpu.CompilerParams(vmem_limit_bytes=VMEM_LIMIT),
        cost_estimate=pl.CostEstimate(
            flops=2 * types * n_others * samples * genes,
            bytes_accessed=2 * samples * genes,
            transcendentals=0,
        ),
        name="first_products",
    )(*parts, mine, others, held)


def second_kernel(types, step, kept, mine, held, cross, left):
    samples = held.shape[0]
    n_mine = mine.shape[0]
    for c in range(samples // step):
        cols = slice(c * step, (c + 1) * step)
        p = kept[:, cols]
        design_rows(left, mine, [p[k : k + 1] for k in range(types)], cols, n_mine)
        out = jnp.dot(left[...], held[cols, :], preferred_element_type=F32)
        if c == 0:
            cross[...] = out
        else:
            cross[...] += out


def second_products(kept, mine, held, types):
    samples, genes = held.shape
    step = 512
    rows = types * mine.shape[0]
    vmem = pl.BlockSpec(memory_space=pltpu.VMEM)
    return pl.pallas_call(
        functools.partial(second_kernel, types, step),
        in_specs=[vmem] * 3,
        out_specs=vmem,
        out_shape=jax.ShapeDtypeStruct((rows, genes), F32),
        scratch_shapes=[pltpu.VMEM((rows, step), BF16)],
        compiler_params=pltpu.CompilerParams(vmem_limit_bytes=VMEM_LIMIT),
        cost_estimate=pl.CostEstimate(
            flops=2 * rows * samples * genes, bytes_accessed=2 * samples * genes, transcendentals=0
        ),
        name="second_products",
    )(kept, mine, held)


def last_kernel(types, scale, own, peers, *refs):
    cross_own, small_own, corr_own = refs[:3]
    rest = refs[3 : 3 + 3 * peers]
    out, turned, ready, sems = refs[3 + 3 * peers :]
    n_mine = corr_own.shape[0]
    genes = cross_own.shape[1]

    small = small_own[...]
    corr = corr_own[...]
    for i in range(peers):
        small = small + rest[3 * i + 1][...]
        corr = corr + rest[3 * i + 2][...]
    corr = corr[:, 0:64] + (corr[:, 64:128] + corr[:, 128:192])
    corr_t = corr.T
    low, inv = cholesky(entries(small[ROWS:, :LANES]), types)
    like = (1, genes)
    low = {key: wide(value, like) for key, value in low.items() if key[0] != key[1]}
    inv = [wide(value, like) for value in inv]
    coef = substitute(low, inv, [small[k : k + 1] for k in range(types)])
    coef = jnp.concatenate(coef + [jnp.zeros((ROWS - types, genes), F32)], axis=0)
    q = split3(coef)
    right = stacked([q[0], q[1], q[2], q[0], q[1], q[0]], 48)
    for k in range(types):
        c = split3(corr_t[ROWS * k : ROWS * (k + 1)])
        turned[:, k * n_mine : (k + 1) * n_mine] = jnp.concatenate(
            [c[0], c[0], c[0], c[1], c[1], c[2]], axis=0
        )
    turned_b = turned[...].astype(BF16)
    copies = []
    for t in range(genes // LANES):
        lanes = slice(t * LANES, (t + 1) * LANES)
        fitted = lax.dot_general(
            turned_b, right[:, lanes], (((0,), (0,)), ((), ())), preferred_element_type=F32
        )
        for k in range(types):
            rows = slice(k * n_mine, k * n_mine + own)
            value = cross_own[rows, lanes]
            for i in range(peers):
                value = value + rest[3 * i][k * own : (k + 1) * own, lanes]
            ready[t, pl.ds(k, own, stride=types), :] = (value - fitted[rows]) * scale
        copy = pltpu.make_async_copy(ready.at[t], out.at[:, pl.ds(t * LANES, LANES)], sems.at[t])
        copy.start()
        copies.append(copy)
    for copy in copies:
        copy.wait()


def finish(cross, small, corr, received, own, types, scale):
    genes = cross.shape[1]
    n_mine = corr.shape[0]
    vmem = pl.BlockSpec(memory_space=pltpu.VMEM)
    flat = [piece for group in received for piece in group]
    return pl.pallas_call(
        functools.partial(last_kernel, types, scale, own, len(received)),
        in_specs=[vmem] * (3 + len(flat)),
        out_specs=pl.BlockSpec(memory_space=pl.ANY),
        out_shape=jax.ShapeDtypeStruct((types * own, genes), F32),
        scratch_shapes=[
            pltpu.VMEM((48, types * n_mine), F32),
            pltpu.VMEM((genes // LANES, types * own, LANES), F32),
            pltpu.SemaphoreType.DMA((genes // LANES,)),
        ],
        compiler_params=pltpu.CompilerParams(vmem_limit_bytes=VMEM_LIMIT),
        name="finish",
    )(cross, small, corr, *flat)


def exchange_all(part, n_gene):
    def swap(offset):
        return lax.ppermute(part, "gene", [(i, i ^ offset) for i in range(n_gene)])

    return (part, swap(1), swap(2), swap(3))


def local(n_gene, n_sample, expression, profile, dosage, signature):
    s_dev, g_dev = expression.shape
    v_dev = dosage.shape[1]
    types = profile.shape[1]
    own = v_dev // n_sample
    scale = 1.0 / math.sqrt(s_dev * n_sample)

    held, part = right_sides(expression, profile.T, signature)
    mine, others = turn_dosage(dosage, own)
    parts = exchange_all(part, n_gene)
    cross_oth, props, kept, small, corr_own, corr_oth = first_products(
        parts, mine, others, held, types
    )
    received = []
    n_mine, n_oth = mine.shape[0], others.shape[0]
    for d in range(1, n_sample):
        pairs = [(i, (i + d) % n_sample) for i in range(n_sample)]
        cross, corr = cross_oth, corr_oth
        if n_oth != own:
            cut = slice((d - 1) * own, d * own)
            cross = cross.reshape(types, n_oth, g_dev)[:, cut].reshape(types * own, g_dev)
            corr = jnp.pad(corr[cut], ((0, n_mine - own), (0, 0)))
        received.append([lax.ppermute(x, "sample", pairs) for x in (cross, small, corr)])
    cross_own = second_products(kept, mine, held, types)
    interaction = finish(cross_own, small, corr_own, received, own, types, scale)
    return interaction, props.T


def solution(mesh):
    placed = (P("sample", "gene"), P("gene", None), P("sample", "variant"), P())
    return jax.shard_map(
        functools.partial(local, mesh.shape["gene"], mesh.shape["sample"]),
        mesh=mesh,
        in_specs=placed,
        out_specs=(P(("variant", "sample"), "gene"), P("sample", None)),
        check_vma=False,
    )
```

time: 113 us -> 30.4 us (0.27)
  matrix products: 38.1 us -> 0 us
  Pallas kernels: 0 us -> 24 us
  blocking collectives: 23.4 us -> 0 us
  local copies, waits for them, and re-layouts: 15.2 us -> 0 us
  between operations: 13.9 us -> 0.69 us
  other arithmetic: 11.6 us -> 0 us
  waiting for transfers between devices: 10.1 us -> 0.4 us
  starting transfers between devices: 0.3 us -> 5.12 us
    dot_general x7 -> x0, matrix products: 36.5 us -> none  [the longest x1 13.5 us: local(): lax.dot_general(design, expression, (((0,), (0,)), ((), ())), preferred_e...]
    pallas_call x0 -> x5, Pallas kernels: none -> 24 us  [the longest x1 7.26 us: right_sides(): pl.pallas_call(functools.partial(rhs_kernel, types, pieces), in_specs=[pl...]
    psum x2 -> x0, blocking collectives: 14.9 us -> none  [the longest x1 11.4 us: local(): gram_all = lax.psum(gram, 'gene')]
    mul x2 -> x0, local copies, waits for them, and re-layouts: 10.5 us -> none  [the longest x1 9.5 us: local(): dosage.astype(jnp.bfloat16)[:, :, None] * rounded[:, None, :]]
    reduce_scatter x2 -> x0, waiting for transfers between devices: 10 us -> none  [the longest x1 9.99 us: local(): rhs_share = lax.psum_scatter(rhs, 'gene', scatter_dimension=1, tiled=True)]
    all_gather x1 -> x0, blocking collectives: 8.57 us -> none  [local(): props_t = lax.all_gather(share_t, 'gene', axis=1, tiled=True)]
    ppermute x0 -> x6, starting transfers between devices: none -> 5.12 us  [the longest x3 4.6 us: swap(): return lax.ppermute(part, 'gene', [(i, i ^ offset) for i in range(n_gene)])]
    another operation x10 -> x0, other arithmetic: 5 us -> none  [the longest x6 2.6 us: chol_solve(): factor = jnp.linalg.cholesky(gram)]
  transfers between devices with their start and end apart: 3 -> 6, of which waited for: 1 -> 2; matrix products, arithmetic and copies ran while one was open for 25% -> 0% of each run, Pallas kernels for 0% -> 30%
where the time goes in v1:
time: 30.4 us; the launch traced here: 30.2 us
  Pallas kernels  24 us (79%)
  starting transfers between devices  5.12 us (17%)
  between operations  0.69 us (2%)
  waiting for transfers between devices  0.4 us (1%)
    pallas_call x1, Pallas kernels, right_sides(): pl.pallas_call(functools.partial(rhs_kernel, types, pieces), in_specs=[pl...  7.26 us
    pallas_call x1, Pallas kernels, first_products(): pl.pallas_call(functools.partial(first_kernel, types, step), in_specs=[vm...  5.9 us
    pallas_call x1, Pallas kernels, turn_dosage(): pl.pallas_call(functools.partial(dosage_kernel, own), grid=(samples // bl...  4.98 us
    ppermute x3, starting transfers between devices, swap(): return lax.ppermute(part, 'gene', [(i, i ^ offset) for i in range(n_gene)])  4.6 us
    pallas_call x1, Pallas kernels, second_products(): pl.pallas_call(functools.partial(second_kernel, types, step), in_specs=[v...  3.94 us
    pallas_call x1, Pallas kernels, finish(): pl.pallas_call(functools.partial(last_kernel, types, scale, own, len(rece...  1.9 us
  transfers between devices with their start and end apart: 6, of which 2 were waited for; matrix products, arithmetic and copies ran while one was open for 0% of the time, Pallas kernels for 30%

profile of v1, /device:TPU:0, one launch (start us, length us, event | category | flops | bytes accessed | tf_op | source)
XLA Modules:
  0.0 30.2 jit_solution(13620508252076851608)
XLA Ops:
  0.6 7.3 %right_sides.1 = (bf16[4096,1024]{1,0:T(8,128)(2,1)S(1)}, f32[232,128]{1,0:T(8,128)S(1)}) custom-call(s32[500]{0:T(512)} %signature_in.1, f32[7,1024]{1,0:T(8,128)} %bitcast.2, bf16[4096,1024]{1,0:T(8,128)(2,1)} %expression.1), custom_call_target="tpu_custom_call" | custom-call | flops 268435456 | bytes 8388608 | tf_op jit(solution)/shard_map/right_sides/pallas_call | solution.py:171
  7.9 4.0 %collective-permute-start.2 = (f32[232,128]{1,0:T(8,128)S(1)}, f32[232,128]{1,0:T(8,128)S(1)}, u32[]{:S(2)}, u32[]{:S(2)}) collective-permute-start(f32[232,128]{1,0:T(8,128)S(1)} %get-tuple-element.12.own_parts), channel_id=1, source_target_pairs={{0,24},{8,16},{16,8},{24,0},{1,25},{9,17},{17,9},{25,1},{2,26},{10... | collective-permute-start | bytes 356360 | tf_op jit(solution)/shard_map/ppermute | solution.py:453
  11.9 0.5 %collective-permute-start.1 = (f32[232,128]{1,0:T(8,128)S(1)}, f32[232,128]{1,0:T(8,128)S(1)}, u32[]{:S(2)}, u32[]{:S(2)}) collective-permute-start(f32[232,128]{1,0:T(8,128)S(1)} %get-tuple-element.12.own_parts), channel_id=1, source_target_pairs={{0,16},{8,24},{16,0},{24,8},{1,17},{9,25},{17,1},{25,9},{2,18},{10... | collective-permute-start | bytes 356360 | tf_op jit(solution)/shard_map/ppermute | solution.py:453
  12.4 0.1 collective-permute-start
  12.5 5.0 %turn_dosage.1 = (bf16[64,4096]{1,0:T(8,128)(2,1)S(1)}, bf16[64,4096]{1,0:T(8,128)(2,1)S(1)}) custom-call(s32[4096,128]{1,0:T(8,128)} %dosage.1), custom_call_target="tpu_custom_call" | custom-call | flops 524288 | bytes 3145728 | tf_op jit(solution)/shard_map/turn_dosage/pallas_call | solution.py:218
  17.5 0.0 collective-permute-done.2.refs_2_
  17.5 0.1 collective-permute-done.1.refs_1_
  17.6 0.2 collective-permute-done.refs_0_
  17.9 5.9 %first_products.1 = (f32[448,1024]{1,0:T(8,128)S(1)}, f32[7,4096]{1,0:T(8,128)}, f32[8,4096]{1,0:T(8,128)S(1)}, f32[16,1024]{1,0:T(8,128)S(1)}, f32[64,192]{1,0:T(8,128)S(1)}, /*index=5*/f32[64,192]{1,0:T(8,128)S(1)}) custom-call(f32[232,128]{1,0:T(8,128)S(1)} %get-tuple-element.12.own_parts, f32[232,128]{1,0:T(8,128)S(1)} %collective-permute-done.refs_0_, ...), custom_call_target="tpu_custom_call" | custom-call | flops 3758096384 | bytes 8388608 | tf_op jit(solution)/shard_map/first_products/pallas_call | solution.py:324
  23.8 0.0 collective-permute-start.3
  23.8 0.5 %collective-permute-start.5 = (f32[64,192]{1,0:T(8,128)S(1)}, f32[64,192]{1,0:T(8,128)S(1)}, u32[]{:S(2)}, u32[]{:S(2)}) collective-permute-start(f32[64,192]{1,0:T(8,128)S(1)} %get-tuple-element.20), channel_id=1, source_target_pairs={{0,4},{4,0},{1,5},{5,1},{2,6},{6,2},{3,7},{7,3},{8,12},{12,8},{9,1... | collective-permute-start | bytes 147464 | tf_op jit(solution)/shard_map/ppermute | solution.py:480
  24.3 0.0 collective-permute-start.4
  24.3 3.9 %second_products.1.refs_0_ = f32[448,1024]{1,0:T(8,128)S(1)} custom-call(f32[8,4096]{1,0:T(8,128)S(1)} %get-tuple-element.16.kept, bf16[64,4096]{1,0:T(8,128)(2,1)S(1)} %get-tuple-element.13.refs_3_.mine, bf16[4096,1024]{1,0:T(8,128)(2,1)S(1)} %get-tuple-element.15.refs_5_.held), custom_call_target="tpu_custom_call" | custom-call | flops 3758096384 | bytes 8388608 | tf_op jit(solution)/shard_map/second_products/pallas_call | solution.py:370
  28.2 0.0 collective-permute-done.5.refs_5_
  28.3 0.0 collective-permute-done.4.refs_4_
  28.3 0.0 collective-permute-done.3.refs_3_
  28.3 1.9 %finish.1 = f32[448,1024]{1,0:T(8,128)} custom-call(f32[448,1024]{1,0:T(8,128)S(1)} %second_products.1.refs_0_, f32[16,1024]{1,0:T(8,128)S(1)} %get-tuple-element.17.refs_1_, f32[64,192]{1,0:T(8,128)S(1)} %get-tuple-element.18.refs_2_, f32[448,1024]{1,0:T(8,128)S(1)} %collective-permute-done.3.refs_3_, f32[16,1024]{1,0:T(8,128)S(1)} %collective-permute-done.4.refs_4_, ...), custom_call_target="tpu_custom_call" | custom-call | tf_op jit(solution)/shard_map/finish/pallas_call | solution.py:436
Async XLA Ops:
  7.9 9.6 %collective-permute-start.2 = (f32[232,128]{1,0:T(8,128)S(1)}, f32[232,128]{1,0:T(8,128)S(1)}, u32[]{:S(2)}, u32[]{:S(2)}) collective-permute-start(f32[232,128]{1,0:T(8,128)S(1)} %get-tuple-element.12.own_parts), channel_id=1, source_target_pairs={{0,24},{8,16},{16,8},{24,0},{1,25},{9,17},{17,9},{25,1},{2,26},{10... | collective-permute-start | bytes 356360 | tf_op jit(solution)/shard_map/ppermute | solution.py:453
  11.9 5.8 %collective-permute-start.1 = (f32[232,128]{1,0:T(8,128)S(1)}, f32[232,128]{1,0:T(8,128)S(1)}, u32[]{:S(2)}, u32[]{:S(2)}) collective-permute-start(f32[232,128]{1,0:T(8,128)S(1)} %get-tuple-element.12.own_parts), channel_id=1, source_target_pairs={{0,16},{8,24},{16,0},{24,8},{1,17},{9,25},{17,1},{25,9},{2,18},{10... | collective-permute-start | bytes 356360 | tf_op jit(solution)/shard_map/ppermute | solution.py:453
  12.4 5.5 %collective-permute-start = (f32[232,128]{1,0:T(8,128)S(1)}, f32[232,128]{1,0:T(8,128)S(1)}, u32[]{:S(2)}, u32[]{:S(2)}) collective-permute-start(f32[232,128]{1,0:T(8,128)S(1)} %get-tuple-element.12.own_parts), channel_id=1, source_target_pairs={{0,8},{8,0},{16,24},{24,16},{1,9},{9,1},{17,25},{25,17},{2,10},{10... | collective-permute-start | bytes 356360 | tf_op jit(solution)/shard_map/ppermute | solution.py:453
  23.8 4.5 %collective-permute-start.3 = (f32[448,1024]{1,0:T(8,128)S(1)}, f32[448,1024]{1,0:T(8,128)S(1)}, u32[]{:S(2)}, u32[]{:S(2)}) collective-permute-start(f32[448,1024]{1,0:T(8,128)S(1)} %get-tuple-element.19), channel_id=1, source_target_pairs={{0,4},{4,0},{1,5},{5,1},{2,6},{6,2},{3,7},{7,3},{8,12},{12,8},{9,1... | collective-permute-start | bytes 5505032 | tf_op jit(solution)/shard_map/ppermute | solution.py:480
  23.8 4.5 %collective-permute-start.5 = (f32[64,192]{1,0:T(8,128)S(1)}, f32[64,192]{1,0:T(8,128)S(1)}, u32[]{:S(2)}, u32[]{:S(2)}) collective-permute-start(f32[64,192]{1,0:T(8,128)S(1)} %get-tuple-element.20), channel_id=1, source_target_pairs={{0,4},{4,0},{1,5},{5,1},{2,6},{6,2},{3,7},{7,3},{8,12},{12,8},{9,1... | collective-permute-start | bytes 147464 | tf_op jit(solution)/shard_map/ppermute | solution.py:480
  24.3 4.0 %collective-permute-start.4 = (f32[16,1024]{1,0:T(8,128)S(1)}, f32[16,1024]{1,0:T(8,128)S(1)}, u32[]{:S(2)}, u32[]{:S(2)}) collective-permute-start(f32[16,1024]{1,0:T(8,128)S(1)} %get-tuple-element.17.refs_1_), channel_id=1, source_target_pairs={{0,4},{4,0},{1,5},{5,1},{2,6},{6,2},{3,7},{7,3},{8,12},{12,8},{9,1... | collective-permute-start | bytes 196616 | tf_op jit(solution)/shard_map/ppermute | solution.py:480

commit v2 on v1

--- a/solution.py
+++ b/solution.py
@@ -54,14 +54,14 @@
         d = entry(j, j)
         for k in range(j):
             d = d - low[j, k] * low[j, k]
-        root = jnp.sqrt(d)
-        low[j, j] = root
-        inv.append(1.0 / root)
+        root = lax.rsqrt(d)
+        root = root * (1.5 - 0.5 * d * root * root)
+        inv.append(root)
         for i in range(j + 1, n):
             v = entry(i, j)
             for k in range(j):
                 v = v - low[i, k] * low[j, k]
-            low[i, j] = v * inv[j]
+            low[i, j] = v * root
     return low, inv
 
 
@@ -166,7 +166,7 @@
 def right_sides(expression, profile_t, signature):
     samples, genes = expression.shape
     types = profile_t.shape[0]
-    pieces = 8
+    pieces = 2
     rows = types * samples // LANES + ROWS
     return pl.pallas_call(
         functools.partial(rhs_kernel, types, pieces),
@@ -190,42 +190,39 @@
     )(in_hbm(signature), in_hbm(profile_t), in_hbm(expression))
 
 
-def dosage_kernel(own, dosage, first, rest):
-    block, variants = dosage.shape
-    wide_d = dosage[...].astype(F32)
-    if own < variants:
-        place = lax.axis_index("sample") * own
-        wide_d = pltpu.roll(wide_d, lax.rem(variants - place, variants), 1)
-    turned = wide_d.T
-    pad = first.shape[0] - own
-    mine = turned[:own]
-    if pad:
-        mine = jnp.concatenate([mine, jnp.zeros((pad, block), F32)], axis=0)
-    first[...] = mine.astype(BF16)
-    left = variants - own
-    if left:
-        others = turned[own:]
-        pad = rest.shape[0] - left
-        if pad:
-            others = jnp.concatenate([others, jnp.zeros((pad, block), F32)], axis=0)
-        rest[...] = others.astype(BF16)
+def dosage_kernel(own, pieces, dosage_in, first, rest, dosage, sems):
+    samples, variants = dosage.shape
+    step = samples // pieces
+    copies = []
+    for i in range(pieces):
+        rows = pl.ds(i * step, step)
+        copy = pltpu.make_async_copy(dosage_in.at[rows], dosage.at[rows], sems.at[i])
+        copy.start()
+        copies.append(copy)
+    shift = lax.rem(variants - lax.axis_index("sample") * own, variants)
+    for i in range(pieces):
+        copies[i].wait()
+        cols = slice(i * step, (i + 1) * step)
+        turned = pltpu.roll(dosage[cols, :].astype(F32), shift, 1).T
+        first[:, cols] = stacked([turned[:own]], first.shape[0])
+        rest[:, cols] = stacked([turned[own:]], rest.shape[0])
 
 
 def turn_dosage(dosage, own):
     samples, variants = dosage.shape
-    block = 512
+    pieces = 4
     first, rest = round_up(own, 16), round_up(variants - own, 16)
     return pl.pallas_call(
-        functools.partial(dosage_kernel, own),
-        grid=(samples // block,),
-        in_specs=[pl.BlockSpec((block, variants), lambda i: (i, 0))],
-        out_specs=[
-            pl.BlockSpec((first, block), lambda i: (0, i)),
-            pl.BlockSpec((rest, block), lambda i: (0, i)),
-        ],
+        functools.partial(dosage_kernel, own, pieces),
+        in_specs=[pl.BlockSpec(memory_space=pltpu.HBM)],
+        out_specs=[pl.BlockSpec(memory_space=pltpu.VMEM)] * 2,
         out_shape=[
-            jax.ShapeDtypeStruct((first, samples), BF16),
-            jax.ShapeDtypeStruct((rest, samples), BF16),
+            pltpu.VMEM((first, samples), BF16),
+            pltpu.VMEM((rest, samples), BF16),
+        ],
+        scratch_shapes=[
+            pltpu.VMEM(dosage.shape, jnp.int32),
+            pltpu.SemaphoreType.DMA((pieces,)),
         ],
         compiler_params=pltpu.CompilerParams(vmem_limit_bytes=VMEM_LIMIT),
         cost_estimate=pl.CostEstimate(
@@ -260,7 +257,7 @@
     gram = total(slice(last, last + ROWS))
     low, inv = cholesky(entries(gram), types)
     like = (groups, LANES)
-    low = {key: wide(value, like) for key, value in low.items() if key[0] != key[1]}
+    low = {key: wide(value, like) for key, value in low.items()}
     inv = [wide(value, like) for value in inv]
     right = [total(pl.ds(k, groups, stride=types)) for k in range(types)]
     solved = substitute(low, inv, right)
@@ -397,7 +394,7 @@
     corr_t = corr.T
     low, inv = cholesky(entries(small[ROWS:, :LANES]), types)
     like = (1, genes)
-    low = {key: wide(value, like) for key, value in low.items() if key[0] != key[1]}
+    low = {key: wide(value, like) for key, value in low.items()}
     inv = [wide(value, like) for value in inv]
     coef = substitute(low, inv, [small[k : k + 1] for k in range(types)])
     coef = jnp.concatenate(coef + [jnp.zeros((ROWS - types, genes), F32)], axis=0)

time: 30.4 us -> 28.7 us (0.944)
  Pallas kernels: 24 us -> 19.3 us
  waiting for transfers between devices: 0.4 us -> 3.37 us
    ppermute x3, waiting for transfers between devices: 0.39 us -> 3.36 us  [swap(): return lax.ppermute(part, 'gene', [(i, i ^ offset) for i in range(n_gene)])]
    pallas_call x1, Pallas kernels: 4.98 us -> 2.01 us  [turn_dosage(): pl.pallas_call(functools.partial(dosage_kernel, own, pieces), in_specs=[p...]
    pallas_call x1, Pallas kernels: 7.26 us -> 5.6 us  [right_sides(): pl.pallas_call(functools.partial(rhs_kernel, types, pieces), in_specs=[pl...]
  transfers between devices with their start and end apart: 6 -> 6, of which waited for: 2 -> 3; matrix products, arithmetic and copies ran while one was open for 0% -> 0% of each run, Pallas kernels for 30% -> 21%
where the time goes in v2:
time: 28.7 us; the launch traced here: 28.5 us
  Pallas kernels  19.3 us (67%)
  starting transfers between devices  5.11 us (18%)
  waiting for transfers between devices  3.37 us (12%)
  between operations  0.68 us (2%)
    pallas_call x1, Pallas kernels, first_products(): pl.pallas_call(functools.partial(first_kernel, types, step), in_specs=[vm...  5.87 us
    pallas_call x1, Pallas kernels, right_sides(): pl.pallas_call(functools.partial(rhs_kernel, types, pieces), in_specs=[pl...  5.6 us
    ppermute x3, starting transfers between devices, swap(): return lax.ppermute(part, 'gene', [(i, i ^ offset) for i in range(n_gene)])  4.6 us
    pallas_call x1, Pallas kernels, second_products(): pl.pallas_call(functools.partial(second_kernel, types, step), in_specs=[v...  3.94 us
    ppermute x3, waiting for transfers between devices, swap(): return lax.ppermute(part, 'gene', [(i, i ^ offset) for i in range(n_gene)])  3.36 us
    pallas_call x1, Pallas kernels, turn_dosage(): pl.pallas_call(functools.partial(dosage_kernel, own, pieces), in_specs=[p...  2.01 us
    pallas_call x1, Pallas kernels, finish(): pl.pallas_call(functools.partial(last_kernel, types, scale, own, len(rece...  1.9 us
  transfers between devices with their start and end apart: 6, of which 3 were waited for; matrix products, arithmetic and copies ran while one was open for 0% of the time, Pallas kernels for 21%

profile of v2, /device:TPU:0, one launch (start us, length us, event | category | flops | bytes accessed | tf_op | source)
XLA Modules:
  0.0 28.5 jit_solution(7391252443273316899)
XLA Ops:
  0.6 5.6 %right_sides.1 = (bf16[4096,1024]{1,0:T(8,128)(2,1)S(1)}, f32[232,128]{1,0:T(8,128)S(1)}) custom-call(s32[500]{0:T(512)} %signature_in.1, f32[7,1024]{1,0:T(8,128)} %bitcast.2, bf16[4096,1024]{1,0:T(8,128)(2,1)} %expression.1), custom_call_target="tpu_custom_call" | custom-call | flops 268435456 | bytes 8388608 | tf_op jit(solution)/shard_map/right_sides/pallas_call | solution.py:171
  6.2 4.0 %collective-permute-start.2 = (f32[232,128]{1,0:T(8,128)S(1)}, f32[232,128]{1,0:T(8,128)S(1)}, u32[]{:S(2)}, u32[]{:S(2)}) collective-permute-start(f32[232,128]{1,0:T(8,128)S(1)} %get-tuple-element.12.own_parts), channel_id=1, source_target_pairs={{0,24},{8,16},{16,8},{24,0},{1,25},{9,17},{17,9},{25,1},{2,26},{10... | collective-permute-start | bytes 356360 | tf_op jit(solution)/shard_map/ppermute | solution.py:450
  10.2 0.5 %collective-permute-start.1 = (f32[232,128]{1,0:T(8,128)S(1)}, f32[232,128]{1,0:T(8,128)S(1)}, u32[]{:S(2)}, u32[]{:S(2)}) collective-permute-start(f32[232,128]{1,0:T(8,128)S(1)} %get-tuple-element.12.own_parts), channel_id=1, source_target_pairs={{0,16},{8,24},{16,0},{24,8},{1,17},{9,25},{17,1},{25,9},{2,18},{10... | collective-permute-start | bytes 356360 | tf_op jit(solution)/shard_map/ppermute | solution.py:450
  10.7 0.1 collective-permute-start
  10.8 2.0 %turn_dosage.1 = (bf16[64,4096]{1,0:T(8,128)(2,1)S(1)}, bf16[64,4096]{1,0:T(8,128)(2,1)S(1)}) custom-call(s32[4096,128]{1,0:T(8,128)} %dosage_in.1), custom_call_target="tpu_custom_call" | custom-call | flops 524288 | bytes 3145728 | tf_op jit(solution)/shard_map/turn_dosage/pallas_call | solution.py:215
  12.9 1.0 %collective-permute-done.2.refs_2_ = f32[232,128]{1,0:T(8,128)S(1)} collective-permute-done((f32[232,128]{1,0:T(8,128)S(1)}, f32[232,128]{1,0:T(8,128)S(1)}, u32[]{:S(2)}, u32[]{:S(2)}) %collective-permute-start.2) | collective-permute-done | bytes 118816 | tf_op jit(solution)/shard_map/ppermute | solution.py:450
  13.8 2.1 %collective-permute-done.1.refs_1_ = f32[232,128]{1,0:T(8,128)S(1)} collective-permute-done((f32[232,128]{1,0:T(8,128)S(1)}, f32[232,128]{1,0:T(8,128)S(1)}, u32[]{:S(2)}, u32[]{:S(2)}) %collective-permute-start.1) | collective-permute-done | bytes 118816 | tf_op jit(solution)/shard_map/ppermute | solution.py:450
  16.0 0.2 collective-permute-done.refs_0_
  16.2 5.9 %first_products.1 = (f32[448,1024]{1,0:T(8,128)S(1)}, f32[7,4096]{1,0:T(8,128)}, f32[8,4096]{1,0:T(8,128)S(1)}, f32[16,1024]{1,0:T(8,128)S(1)}, f32[64,192]{1,0:T(8,128)S(1)}, /*index=5*/f32[64,192]{1,0:T(8,128)S(1)}) custom-call(f32[232,128]{1,0:T(8,128)S(1)} %get-tuple-element.12.own_parts, f32[232,128]{1,0:T(8,128)S(1)} %collective-permute-done.refs_0_, ...), custom_call_target="tpu_custom_call" | custom-call | flops 3758096384 | bytes 8388608 | tf_op jit(solution)/shard_map/first_products/pallas_call | solution.py:321
  22.1 0.0 collective-permute-start.3
  22.1 0.5 %collective-permute-start.5 = (f32[64,192]{1,0:T(8,128)S(1)}, f32[64,192]{1,0:T(8,128)S(1)}, u32[]{:S(2)}, u32[]{:S(2)}) collective-permute-start(f32[64,192]{1,0:T(8,128)S(1)} %get-tuple-element.20), channel_id=1, source_target_pairs={{0,4},{4,0},{1,5},{5,1},{2,6},{6,2},{3,7},{7,3},{8,12},{12,8},{9,1... | collective-permute-start | bytes 147464 | tf_op jit(solution)/shard_map/ppermute | solution.py:477
  22.6 0.0 collective-permute-start.4
  22.6 3.9 %second_products.1.refs_0_ = f32[448,1024]{1,0:T(8,128)S(1)} custom-call(f32[8,4096]{1,0:T(8,128)S(1)} %get-tuple-element.16.kept, bf16[64,4096]{1,0:T(8,128)(2,1)S(1)} %get-tuple-element.13.refs_3_.mine, bf16[4096,1024]{1,0:T(8,128)(2,1)S(1)} %get-tuple-element.15.refs_5_.held), custom_call_target="tpu_custom_call" | custom-call | flops 3758096384 | bytes 8388608 | tf_op jit(solution)/shard_map/second_products/pallas_call | solution.py:367
  26.6 0.0 collective-permute-done.5.refs_5_
  26.6 0.0 collective-permute-done.4.refs_4_
  26.6 0.0 collective-permute-done.3.refs_3_
  26.6 1.9 %finish.1 = f32[448,1024]{1,0:T(8,128)} custom-call(f32[448,1024]{1,0:T(8,128)S(1)} %second_products.1.refs_0_, f32[16,1024]{1,0:T(8,128)S(1)} %get-tuple-element.17.refs_1_, f32[64,192]{1,0:T(8,128)S(1)} %get-tuple-element.18.refs_2_, f32[448,1024]{1,0:T(8,128)S(1)} %collective-permute-done.3.refs_3_, f32[16,1024]{1,0:T(8,128)S(1)} %collective-permute-done.4.refs_4_, ...), custom_call_target="tpu_custom_call" | custom-call | tf_op jit(solution)/shard_map/finish/pallas_call | solution.py:433
Async XLA Ops:
  6.2 7.6 %collective-permute-start.2 = (f32[232,128]{1,0:T(8,128)S(1)}, f32[232,128]{1,0:T(8,128)S(1)}, u32[]{:S(2)}, u32[]{:S(2)}) collective-permute-start(f32[232,128]{1,0:T(8,128)S(1)} %get-tuple-element.12.own_parts), channel_id=1, source_target_pairs={{0,24},{8,16},{16,8},{24,0},{1,25},{9,17},{17,9},{25,1},{2,26},{10... | collective-permute-start | bytes 356360 | tf_op jit(solution)/shard_map/ppermute | solution.py:450
  10.2 5.8 %collective-permute-start.1 = (f32[232,128]{1,0:T(8,128)S(1)}, f32[232,128]{1,0:T(8,128)S(1)}, u32[]{:S(2)}, u32[]{:S(2)}) collective-permute-start(f32[232,128]{1,0:T(8,128)S(1)} %get-tuple-element.12.own_parts), channel_id=1, source_target_pairs={{0,16},{8,24},{16,0},{24,8},{1,17},{9,25},{17,1},{25,9},{2,18},{10... | collective-permute-start | bytes 356360 | tf_op jit(solution)/shard_map/ppermute | solution.py:450
  10.7 5.5 %collective-permute-start = (f32[232,128]{1,0:T(8,128)S(1)}, f32[232,128]{1,0:T(8,128)S(1)}, u32[]{:S(2)}, u32[]{:S(2)}) collective-permute-start(f32[232,128]{1,0:T(8,128)S(1)} %get-tuple-element.12.own_parts), channel_id=1, source_target_pairs={{0,8},{8,0},{16,24},{24,16},{1,9},{9,1},{17,25},{25,17},{2,10},{10... | collective-permute-start | bytes 356360 | tf_op jit(solution)/shard_map/ppermute | solution.py:450
  22.1 4.5 %collective-permute-start.3 = (f32[448,1024]{1,0:T(8,128)S(1)}, f32[448,1024]{1,0:T(8,128)S(1)}, u32[]{:S(2)}, u32[]{:S(2)}) collective-permute-start(f32[448,1024]{1,0:T(8,128)S(1)} %get-tuple-element.19), channel_id=1, source_target_pairs={{0,4},{4,0},{1,5},{5,1},{2,6},{6,2},{3,7},{7,3},{8,12},{12,8},{9,1... | collective-permute-start | bytes 5505032 | tf_op jit(solution)/shard_map/ppermute | solution.py:477
  22.1 4.5 %collective-permute-start.5 = (f32[64,192]{1,0:T(8,128)S(1)}, f32[64,192]{1,0:T(8,128)S(1)}, u32[]{:S(2)}, u32[]{:S(2)}) collective-permute-start(f32[64,192]{1,0:T(8,128)S(1)} %get-tuple-element.20), channel_id=1, source_target_pairs={{0,4},{4,0},{1,5},{5,1},{2,6},{6,2},{3,7},{7,3},{8,12},{12,8},{9,1... | collective-permute-start | bytes 147464 | tf_op jit(solution)/shard_map/ppermute | solution.py:477
  22.6 4.0 %collective-permute-start.4 = (f32[16,1024]{1,0:T(8,128)S(1)}, f32[16,1024]{1,0:T(8,128)S(1)}, u32[]{:S(2)}, u32[]{:S(2)}) collective-permute-start(f32[16,1024]{1,0:T(8,128)S(1)} %get-tuple-element.17.refs_1_), channel_id=1, source_target_pairs={{0,4},{4,0},{1,5},{5,1},{2,6},{6,2},{3,7},{7,3},{8,12},{12,8},{9,1... | collective-permute-start | bytes 196616 | tf_op jit(solution)/shard_map/ppermute | solution.py:477

commit v3 on v2

v3 whole, which is shorter than its diff:
```python
import functools
import math

import jax
import jax.numpy as jnp
from jax import lax
from jax.experimental import pallas as pl
from jax.experimental.pallas import tpu as pltpu
from jax.sharding import PartitionSpec as P

F32 = jnp.float32
BF16 = jnp.bfloat16
VMEM_LIMIT = 32 << 20
LANES = 128
ROWS = 8
RHS_PIECES = 2


def round_up(n, m):
    return (n + m - 1) // m * m


def in_hbm(x):
    return pltpu.with_memory_space_constraint(x, pltpu.HBM)


def split3(x):
    hi = x.astype(BF16).astype(F32)
    rest = x - hi
    mid = rest.astype(BF16).astype(F32)
    return hi, mid, rest - mid


def stacked(parts, rows):
    have = sum(p.shape[0] for p in parts)
    if have < rows:
        parts = list(parts) + [jnp.zeros((rows - have, parts[0].shape[1]), F32)]
    return jnp.concatenate(parts, axis=0).astype(BF16)


def cholesky(entry, n):
    low = {}
    inv = []
    for j in range(n):
        d = entry(j, j)
        for k in range(j):
            d = d - low[j, k] * low[j, k]
        root = lax.rsqrt(d)
        root = root * (1.5 - 0.5 * d * root * root)
        inv.append(root)
        for i in range(j + 1, n):
            v = entry(i, j)
            for k in range(j):
                v = v - low[i, k] * low[j, k]
            low[i, j] = v * root
    return low, inv


def substitute(low, inv, right):
    n = len(right)
    y = []
    for i in range(n):
        v = right[i]
        for k in range(i):
            v = v - low[i, k] * y[k]
        y.append(v * inv[i])
    x = [None] * n
    for i in reversed(range(n)):
        v = y[i]
        for k in range(i + 1, n):
            v = v - low[k, i] * x[k]
        x[i] = v * inv[i]
    return x


def entries(tile):
    cache = {}

    def entry(i, j):
        if (i, j) not in cache:
            cache[i, j] = jnp.broadcast_to(tile[i : i + 1, j : j + 1], (ROWS, LANES))
        return cache[i, j]

    return entry


def inner_products(x, n):
    col = lax.broadcasted_iota(jnp.int32, (ROWS, LANES), 1)
    out = jnp.zeros((ROWS, LANES), F32)
    for j in range(n):
        out = jnp.where(col == j, jnp.sum(x * x[j : j + 1], axis=1, keepdims=True), out)
    return out


def wide(tile, like):
    rows, cols = like
    if rows == 1:
        return jnp.concatenate([tile[0:1]] * (cols // LANES), axis=1)
    return jnp.concatenate([tile] * (rows // ROWS), axis=0)


def rhs_kernel(
    types, halves, pieces, signature_in, profile_in, expression, held, parts, signature, profile, sems, few
):
    samples, genes = held.shape
    step = samples // pieces
    early = [
        pltpu.make_async_copy(signature_in, signature, few.at[0]),
        pltpu.make_async_copy(profile_in, profile, few.at[1]),
    ]
    for copy in early:
        copy.start()
    start = lax.rem(lax.axis_index("variant"), halves) * samples
    copies = []
    for i in range(pieces):
        rows = pl.ds(i * step, step)
        there = pl.ds(pl.multiple_of(start + i * step, step), step)
        copy = pltpu.make_async_copy(expression.at[there], held.at[rows], sems.at[i])
        copy.start()
        copies.append(copy)

    for copy in early:
        copy.wait()
    groups = genes // LANES
    base = lax.axis_index("gene") * genes
    shape = (groups, LANES)
    ids = (
        base
        + lax.broadcasted_iota(jnp.int32, shape, 0) * LANES
        + lax.broadcasted_iota(jnp.int32, shape, 1)
    )

    n_sig = signature.shape[0]
    unroll = 10 if n_sig % 10 == 0 else 1

    def look(i, member):
        for u in range(unroll):
            member = member | (ids == signature[i * unroll + u]).astype(jnp.int32)
        return member

    member = lax.fori_loop(0, n_sig // unroll, look, jnp.zeros(shape, jnp.int32))
    member = (member > 0).astype(F32)
    row = jnp.concatenate([member[h : h + 1] for h in range(groups)], axis=1)
    masked = profile[...] * row
    masked = jnp.concatenate([masked, jnp.zeros((ROWS - types, genes), F32)], axis=0)
    left = stacked(split3(masked), 32)
    parts[types * samples // LANES :, :] = inner_products(masked, types)

    for i in range(pieces):
        copies[i].wait()
        out = lax.dot_general(
            left,
            held[i * step : (i + 1) * step, :],
            (((1,), (1,)), ((), ())),
            preferred_element_type=F32,
        )
        out = out[0:ROWS] + (out[ROWS : 2 * ROWS] + out[2 * ROWS : 3 * ROWS])
        for c in range(step // LANES):
            at = (i * step // LANES + c) * types
            parts[at : at + types, :] = out[:types, c * LANES : (c + 1) * LANES]


def right_sides(expression, profile_t, signature, halves):
    samples, genes = expression.shape
    samples = samples // halves
    types = profile_t.shape[0]
    pieces = RHS_PIECES
    rows = types * samples // LANES + ROWS
    return pl.pallas_call(
        functools.partial(rhs_kernel, types, halves, pieces),
        in_specs=[pl.BlockSpec(memory_space=pltpu.HBM)] * 3,
        out_specs=[pl.BlockSpec(memory_space=pltpu.VMEM)] * 2,
        out_shape=[
            pltpu.VMEM((samples, genes), BF16),
            jax.ShapeDtypeStruct((rows, LANES), F32),
        ],
        scratch_shapes=[
            pltpu.SMEM(signature.shape, jnp.int32),
            pltpu.VMEM(profile_t.shape, F32),
            pltpu.SemaphoreType.DMA((pieces,)),
            pltpu.SemaphoreType.DMA((2,)),
        ],
        compiler_params=pltpu.CompilerParams(vmem_limit_bytes=VMEM_LIMIT),
        cost_estimate=pl.CostEstimate(
            flops=2 * 32 * samples * genes, bytes_accessed=2 * samples * genes, transcendentals=0
        ),
        name="right_sides",
    )(in_hbm(signature), in_hbm(profile_t), in_hbm(expression))


def prepare_kernel(own, halves, pieces, dosage_in, expression, first, rest, *refs):
    held = refs[:-3]
    dosage, sems, far_sem = refs[-3:]
    samples, variants = dosage.shape
    half = samples // halves
    step = samples // pieces
    side = lax.rem(lax.axis_index("variant"), halves)
    copies = []
    for i in range(pieces):
        near = i * step // half
        begin = lax.rem(side + near, halves) * half + (i * step - near * half)
        there = pl.ds(pl.multiple_of(begin, step), step)
        copy = pltpu.make_async_copy(dosage_in.at[there], dosage.at[pl.ds(i * step, step)], sems.at[i])
        copy.start()
        copies.append(copy)
    far = []
    for ref in held:
        there = pl.ds(pl.multiple_of((1 - side) * half, half), half)
        copy = pltpu.make_async_copy(expression.at[there], ref, far_sem)
        copy.start()
        far.append(copy)
    shift = lax.rem(variants - lax.axis_index("sample") * own, variants)
    for i in range(pieces):
        copies[i].wait()
        cols = slice(i * step, (i + 1) * step)
        turned = pltpu.roll(dosage[cols, :].astype(F32), shift, 1).T
        first[:, cols] = stacked([turned[:own]], first.shape[0])
        rest[:, cols] = stacked([turned[own:]], rest.shape[0])
    for copy in far:
        copy.wait()


def prepare(dosage, expression, own, halves):
    samples, variants = dosage.shape
    genes = expression.shape[1]
    pieces = 4
    first, rest = round_up(own, 16), round_up(variants - own, 16)
    return pl.pallas_call(
        functools.partial(prepare_kernel, own, halves, pieces),
        in_specs=[pl.BlockSpec(memory_space=pltpu.HBM)] * 2,
        out_specs=[pl.BlockSpec(memory_space=pltpu.VMEM)] * (1 + halves),
        out_shape=[pltpu.VMEM((first, samples), BF16), pltpu.VMEM((rest, samples), BF16)]
        + [pltpu.VMEM((samples // halves, genes), BF16)] * (halves - 1),
        scratch_shapes=[
            pltpu.VMEM(dosage.shape, jnp.int32),
            pltpu.SemaphoreType.DMA((pieces,)),
            pltpu.SemaphoreType.DMA,
        ],
        compiler_params=pltpu.CompilerParams(vmem_limit_bytes=VMEM_LIMIT),
        cost_estimate=pl.CostEstimate(
            flops=samples * variants, bytes_accessed=6 * samples * variants, transcendentals=0
        ),
        name="prepare",
    )(in_hbm(dosage), in_hbm(expression))


def solve_kernel(types, own_parts, x_parts, y_parts, d_parts, solved, packed):
    groups = (own_parts.shape[0] - ROWS) // types
    last = types * groups

    def total(rows):
        return (own_parts[rows, :] + x_parts[rows, :]) + (y_parts[rows, :] + d_parts[rows, :])

    low, inv = cholesky(entries(total(slice(last, last + ROWS))), types)
    like = (groups, LANES)
    low = {key: wide(value, like) for key, value in low.items()}
    inv = [wide(value, like) for value in inv]
    x = substitute(low, inv, [total(pl.ds(k, groups, stride=types)) for k in range(types)])
    for k in range(types):
        packed[pl.ds(k, groups, stride=ROWS), :] = x[k]
    for k in range(types, ROWS):
        packed[pl.ds(k, groups, stride=ROWS), :] = jnp.zeros(like, F32)
    for g in range(groups):
        solved[:, g * LANES : (g + 1) * LANES] = packed[g * ROWS : (g + 1) * ROWS, :]


def solve(parts, types):
    groups = (parts[0].shape[0] - ROWS) // types
    vmem = pl.BlockSpec(memory_space=pltpu.VMEM)
    return pl.pallas_call(
        functools.partial(solve_kernel, types),
        in_specs=[vmem] * 4,
        out_specs=vmem,
        out_shape=jax.ShapeDtypeStruct((ROWS, groups * LANES), F32),
        scratch_shapes=[pltpu.VMEM((groups * ROWS, LANES), F32)],
        compiler_params=pltpu.CompilerParams(vmem_limit_bytes=VMEM_LIMIT),
        name="solve",
    )(*parts)


def design_rows(left, dosage, rounded, cols, count):
    types = len(rounded)
    width = rounded[0].shape[1]
    for k in range(types):
        spread = jnp.broadcast_to(rounded[k], (16, width)).astype(BF16)
        for q in range(count // 16):
            at = k * count + q * 16
            left[at : at + 16, :] = dosage[q * 16 : q * 16 + 16, cols] * spread


def others_kernel(types, step, first_col, has_before, *refs):
    p_in, mine, others, held = refs[:4]
    before = refs[4:8] if has_before else None
    cross, small, corr_own, corr_oth, left, weights = refs[-6:]
    samples, genes = held.shape
    n_rows = types * others.shape[0]

    pp = inner_products(p_in[...], types)
    small[ROWS:, :] = jnp.concatenate([pp, jnp.zeros((ROWS, genes - LANES), F32)], axis=1)
    if has_before:
        small[ROWS:, :LANES] += before[1][ROWS:, :LANES]

    for c in range(samples // step):
        here = slice(c * step, (c + 1) * step)
        cols = slice(first_col + c * step, first_col + (c + 1) * step)
        p = p_in[:, here]
        pieces = split3(p)
        rounded = [pieces[0][k : k + 1] for k in range(types)]
        design_rows(left, others, rounded, cols, others.shape[0])
        left[n_rows:, :] = stacked(pieces, 32)
        w_parts = split3(jnp.concatenate([r * p for r in rounded], axis=0))
        for s in range(3):
            weights[s * 64 : s * 64 + 64, :] = stacked([w_parts[s]], 64)
        out = jnp.dot(left[...], held[here, :], preferred_element_type=F32)
        contract = (((1,), (1,)), ((), ()))
        co = lax.dot_general(others[:, cols], weights[...], contract, preferred_element_type=F32)
        cm = lax.dot_general(mine[:, cols], weights[...], contract, preferred_element_type=F32)
        py = out[n_rows : n_rows + ROWS] + (
            out[n_rows + ROWS : n_rows + 2 * ROWS] + out[n_rows + 2 * ROWS : n_rows + 3 * ROWS]
        )
        old = None
        if c:
            old = (cross, small, corr_own, corr_oth)
        elif has_before:
            old = before
        if old is None:
            cross[...] = out[:n_rows]
            small[:ROWS, :] = py
            corr_own[...] = cm
            corr_oth[...] = co
        else:
            cross[...] = old[0][...] + out[:n_rows]
            small[:ROWS, :] = old[1][:ROWS, :] + py
            corr_own[...] = old[2][...] + cm
            corr_oth[...] = old[3][...] + co


def others_products(p, mine, others, held, first_col, before, types):
    samples, genes = held.shape
    step = 512
    n_mine, n_others = mine.shape[0], others.shape[0]
    vmem = pl.BlockSpec(memory_space=pltpu.VMEM)
    before = list(before or [])
    return pl.pallas_call(
        functools.partial(others_kernel, types, step, first_col, bool(before)),
        in_specs=[vmem] * (4 + len(before)),
        out_specs=[vmem] * 4,
        out_shape=[
            jax.ShapeDtypeStruct((types * n_others, genes), F32),
            jax.ShapeDtypeStruct((2 * ROWS, genes), F32),
            jax.ShapeDtypeStruct((n_mine, 192), F32),
            jax.ShapeDtypeStruct((n_others, 192), F32),
        ],
        scratch_shapes=[
            pltpu.VMEM((types * n_others + 32, step), BF16),
            pltpu.VMEM((192, step), BF16),
        ],
        compiler_params=pltpu.CompilerParams(vmem_limit_bytes=VMEM_LIMIT),
        cost_estimate=pl.CostEstimate(
            flops=2 * types * n_others * samples * genes,
            bytes_accessed=2 * samples * genes,
            transcendentals=0,
        ),
        name="others_products",
    )(p, mine, others, held, *before)


def own_dot(types, step, p_in, mine, held, lanes, left, add):
    first_col = 0
    first = True
    for p_ref, held_ref in zip(p_in, held):
        samples = held_ref.shape[0]
        for c in range(samples // step):
            here = slice(c * step, (c + 1) * step)
            cols = slice(first_col + c * step, first_col + (c + 1) * step)
            rounded = p_ref[:, here].astype(BF16).astype(F32)
            design_rows(left, mine, [rounded[k : k + 1] for k in range(types)], cols, mine.shape[0])
            add(jnp.dot(left[...], held_ref[here, lanes], preferred_element_type=F32), first)
            first = False
        first_col += samples


def own_kernel(types, step, halves, *refs):
    p_in, held, mine = refs[:halves], refs[halves : 2 * halves], refs[2 * halves]
    cross, props, left = refs[2 * halves + 1 :]
    half = p_in[0].shape[1]
    side = lax.rem(lax.axis_index("variant"), halves)
    for i in range(halves):
        at = pl.multiple_of(lax.rem(side + i, halves) * half, half)
        props[:, pl.ds(at, half)] = p_in[i][:types, :]

    def add(out, first):
        if first:
            cross[...] = out
        else:
            cross[...] += out

    own_dot(types, step, p_in, mine, held, slice(0, cross.shape[1]), left, add)


def own_products(p, mine, held, columns, types):
    halves = len(p)
    samples = halves * p[0].shape[1]
    step = 512
    rows = types * mine.shape[0]
    vmem = pl.BlockSpec(memory_space=pltpu.VMEM)
    return pl.pallas_call(
        functools.partial(own_kernel, types, step, halves),
        in_specs=[vmem] * (2 * halves + 1),
        out_specs=[vmem] * 2,
        out_shape=[
            jax.ShapeDtypeStruct((rows, columns), F32),
            jax.ShapeDtypeStruct((types, samples), F32),
        ],
        scratch_shapes=[pltpu.VMEM((rows, step), BF16)],
        compiler_params=pltpu.CompilerParams(vmem_limit_bytes=VMEM_LIMIT),
        cost_estimate=pl.CostEstimate(
            flops=2 * rows * samples * columns, bytes_accessed=2 * samples * columns, transcendentals=0
        ),
        name="own_products",
    )(*p, *held, mine)


def finish_kernel(types, step, scale, own, halves, peers, *refs):
    p_in, held, mine = refs[:halves], refs[halves : 2 * halves], refs[2 * halves]
    before = refs[2 * halves + 1]
    refs = refs[2 * halves + 2 :]
    smalls, corrs, blocks = refs[: 1 + peers], refs[1 + peers : 2 + 2 * peers], refs[2 + 2 * peers : 2 + 3 * peers]
    out, left, turned, last, ready, sems = refs[2 + 3 * peers :]
    n_mine = mine.shape[0]
    genes, columns = held[0].shape[1], before.shape[1]

    small = smalls[0][...]
    corr = corrs[0][...]
    for i in range(peers):
        small = small + smalls[1 + i][...]
        corr = corr + corrs[1 + i][...]
    corr = corr[:, 0:64] + (corr[:, 64:128] + corr[:, 128:192])
    corr_t = corr.T
    low, inv = cholesky(entries(small[ROWS:, :LANES]), types)
    like = (1, genes)
    low = {key: wide(value, like) for key, value in low.items()}
    inv = [wide(value, like) for value in inv]
    coef = substitute(low, inv, [small[k : k + 1] for k in range(types)])
    coef = jnp.concatenate(coef + [jnp.zeros((ROWS - types, genes), F32)], axis=0)
    q = split3(coef)
    right = stacked([q[0], q[1], q[2], q[0], q[1], q[0]], 48)
    for k in range(types):
        c = split3(corr_t[ROWS * k : ROWS * (k + 1)])
        turned[:, k * n_mine : (k + 1) * n_mine] = jnp.concatenate(
            [c[0], c[0], c[0], c[1], c[1], c[2]], axis=0
        )
    turned_b = turned[...].astype(BF16)
    copies = []

    def write(source, begin, end):
        fitted = lax.dot_general(
            turned_b, right[:, begin:end], (((0,), (0,)), ((), ())), preferred_element_type=F32
        )
        for t in range(begin // LANES, end // LANES):
            lanes = slice(t * LANES, (t + 1) * LANES)
            here = slice(t * LANES - begin, (t + 1) * LANES - begin)
            for k in range(types):
                rows = slice(k * n_mine, k * n_mine + own)
                value = source[rows, here] - fitted[rows, here]
                for block in blocks:
                    value = value + block[k * own : (k + 1) * own, lanes]
                ready[t, pl.ds(k, own, stride=types), :] = value * scale
            copy = pltpu.make_async_copy(ready.at[t], out.at[:, pl.ds(t * LANES, LANES)], sems.at[t])
            copy.start()
            copies.append(copy)

    write(before, 0, columns)

    def add(out, first):
        if first:
            last[...] = out
        else:
            last[...] += out

    own_dot(types, step, p_in, mine, held, slice(columns, genes), left, add)
    write(last, columns, genes)
    for copy in copies:
        copy.wait()


def finish(p, mine, held, before, smalls, corrs, blocks, own, types, scale):
    halves = len(p)
    genes, columns = held[0].shape[1], before.shape[1]
    step = 512
    rows = types * mine.shape[0]
    vmem = pl.BlockSpec(memory_space=pltpu.VMEM)
    return pl.pallas_call(
        functools.partial(finish_kernel, types, step, scale, own, halves, len(blocks)),
        in_specs=[vmem] * (2 * halves + 2 + 2 * len(smalls) + len(blocks)),
        out_specs=pl.BlockSpec(memory_space=pl.ANY),
        out_shape=jax.ShapeDtypeStruct((types * own, genes), F32),
        scratch_shapes=[
            pltpu.VMEM((rows, step), BF16),
            pltpu.VMEM((48, rows), F32),
            pltpu.VMEM((rows, genes - columns), F32),
            pltpu.VMEM((genes // LANES, types * own, LANES), F32),
            pltpu.SemaphoreType.DMA((genes // LANES,)),
        ],
        compiler_params=pltpu.CompilerParams(vmem_limit_bytes=VMEM_LIMIT),
        name="finish",
    )(*p, *held, mine, before, *smalls, *corrs, *blocks)


def exchange_all(part, n_gene):
    def swap(offset):
        return lax.ppermute(part, "gene", [(i, i ^ offset) for i in range(n_gene)])

    return (part, swap(2), swap(3), swap(1))


def local(n_gene, n_sample, n_variant, expression, profile, dosage, signature):
    s_dev, g_dev = expression.shape
    v_dev = dosage.shape[1]
    types = profile.shape[1]
    own = v_dev // n_sample
    scale = 1.0 / math.sqrt(s_dev * n_sample)
    halves = 2 if n_variant % 2 == 0 else 1
    half = s_dev // halves

    held, part = right_sides(expression, profile.T, signature, halves)
    parts = exchange_all(part, n_gene)
    mine, others, *far = prepare(dosage, expression, own, halves)
    held = [held] + far
    solved = [solve(parts, types)]
    if halves == 2:
        pairs = [(i, i ^ 1) for i in range(n_variant)]
        solved.append(lax.ppermute(solved[0], "variant", pairs))
    sums = None
    for i in range(halves):
        sums = others_products(solved[i], mine, others, held[i], i * half, sums, types)
    cross_oth, small, corr_own, corr_oth = sums
    n_mine, n_oth = mine.shape[0], others.shape[0]
    blocks, smalls, corrs = [], [small], [corr_own]
    for d in range(1, n_sample):
        pairs = [(i, (i + d) % n_sample) for i in range(n_sample)]
        cross, corr = cross_oth, corr_oth
        if n_oth != own:
            cut = slice((d - 1) * own, d * own)
            cross = cross.reshape(types, n_oth, g_dev)[:, cut].reshape(types * own, g_dev)
            corr = jnp.pad(corr[cut], ((0, n_mine - own), (0, 0)))
        smalls.append(lax.ppermute(small, "sample", pairs))
        corrs.append(lax.ppermute(corr, "sample", pairs))
        blocks.append(lax.ppermute(cross, "sample", pairs))
    columns = g_dev * 3 // 4 // LANES * LANES
    before, props_t = own_products(solved, mine, held, columns, types)
    interaction = finish(
        solved, mine, held, before, smalls, corrs, blocks, own, types, scale
    )
    return interaction, props_t.T


def solution(mesh):
    placed = (P("sample", "gene"), P("gene", None), P("sample", "variant"), P())
    sizes = [mesh.shape[axis] for axis in ("gene", "sample", "variant")]
    return jax.shard_map(
        functools.partial(local, *sizes),
        mesh=mesh,
        in_specs=placed,
        out_specs=(P(("variant", "sample"), "gene"), P("sample", None)),
        check_vma=False,
    )
```

time: 28.7 us -> 26.9 us (0.937)
  waiting for transfers between devices: 3.37 us -> 1.28 us
  starting transfers between devices: 5.11 us -> 6.86 us
  Pallas kernels: 19.3 us -> 17.9 us
    ppermute x3, waiting for transfers between devices: 3.36 us -> 1.21 us  [swap(): return lax.ppermute(part, 'gene', [(i, i ^ offset) for i in range(n_gene)])]
    ppermute x3 -> x4, starting transfers between devices: 0.51 us -> 2.28 us  [the longest x1 1.64 us: local(): solved.append(lax.ppermute(solved[0], 'variant', pairs))]
    pallas_call x5 -> x7, Pallas kernels: 19.3 us -> 17.9 us  [the longest x2 5.27 us: others_products(): pl.pallas_call(functools.partial(others_kernel, types, step, first_col, b...]
  transfers between devices with their start and end apart: 6 -> 7, of which waited for: 3 -> 3; matrix products, arithmetic and copies ran while one was open for 0% -> 0% of each run, Pallas kernels for 21% -> 34%
where the time goes in v3:
time: 26.9 us; the launch traced here: 26.7 us
  Pallas kernels  17.9 us (67%)
  starting transfers between devices  6.86 us (26%)
  waiting for transfers between devices  1.28 us (5%)
  between operations  0.68 us (3%)
    pallas_call x2, Pallas kernels, others_products(): pl.pallas_call(functools.partial(others_kernel, types, step, first_col, b...  5.27 us
    ppermute x3, starting transfers between devices, swap(): return lax.ppermute(part, 'gene', [(i, i ^ offset) for i in range(n_gene)])  4.57 us
    pallas_call x1, Pallas kernels, own_products(): pl.pallas_call(functools.partial(own_kernel, types, step, halves), in_spe...  3.62 us
    pallas_call x1, Pallas kernels, right_sides(): pl.pallas_call(functools.partial(rhs_kernel, types, halves, pieces), in_s...  3.12 us
    pallas_call x1, Pallas kernels, prepare(): pl.pallas_call(functools.partial(prepare_kernel, own, halves, pieces), in...  2.88 us
    pallas_call x1, Pallas kernels, finish(): pl.pallas_call(functools.partial(finish_kernel, types, step, scale, own,...  2.75 us
    ppermute x1, starting transfers between devices, local(): solved.append(lax.ppermute(solved[0], 'variant', pairs))  1.64 us
    ppermute x3, waiting for transfers between devices, swap(): return lax.ppermute(part, 'gene', [(i, i ^ offset) for i in range(n_gene)])  1.21 us
  transfers between devices with their start and end apart: 7, of which 3 were waited for; matrix products, arithmetic and copies ran while one was open for 0% of the time, Pallas kernels for 34%

profile of v3, /device:TPU:0, one launch (start us, length us, event | category | flops | bytes accessed | tf_op | source)
XLA Modules:
  0.0 26.7 jit_solution(9596704005136563004)
XLA Ops:
  0.6 3.1 %right_sides.1 = (bf16[2048,1024]{1,0:T(8,128)(2,1)S(1)}, f32[120,128]{1,0:T(8,128)S(1)}) custom-call(s32[500]{0:T(512)} %signature_in.1, f32[7,1024]{1,0:T(8,128)} %bitcast.2, bf16[4096,1024]{1,0:T(8,128)(2,1)} %expression.3), custom_call_target="tpu_custom_call" | custom-call | flops 134217728 | bytes 4194304 | tf_op jit(solution)/shard_map/right_sides/pallas_call | solution.py:169
  3.8 3.0 %collective-permute-start = (f32[120,128]{1,0:T(8,128)S(1)}, f32[120,128]{1,0:T(8,128)S(1)}, u32[]{:S(2)}, u32[]{:S(2)}) collective-permute-start(f32[120,128]{1,0:T(8,128)S(1)} %get-tuple-element.17.own_parts), channel_id=1, source_target_pairs={{0,16},{8,24},{16,0},{24,8},{1,17},{9,25},{17,1},{25,9},{2,18},{10... | collective-permute-start | bytes 184328 | tf_op jit(solution)/shard_map/ppermute | solution.py:512
  6.8 1.4 %collective-permute-start.1 = (f32[120,128]{1,0:T(8,128)S(1)}, f32[120,128]{1,0:T(8,128)S(1)}, u32[]{:S(2)}, u32[]{:S(2)}) collective-permute-start(f32[120,128]{1,0:T(8,128)S(1)} %get-tuple-element.17.own_parts), channel_id=1, source_target_pairs={{0,24},{8,16},{16,8},{24,0},{1,25},{9,17},{17,9},{25,1},{2,26},{10... | collective-permute-start | bytes 184328 | tf_op jit(solution)/shard_map/ppermute | solution.py:512
  8.2 0.1 collective-permute-start.2
  8.3 2.9 %prepare.1 = (bf16[64,4096]{1,0:T(8,128)(2,1)S(1)}, bf16[64,4096]{1,0:T(8,128)(2,1)S(1)}, bf16[2048,1024]{1,0:T(8,128)(2,1)S(1)}) custom-call(s32[4096,128]{1,0:T(8,128)} %dosage_in.1, bf16[4096,1024]{1,0:T(8,128)(2,1)} %expression.3), custom_call_target="tpu_custom_call" | custom-call | flops 524288 | bytes 3145728 | tf_op jit(solution)/shard_map/prepare/pallas_call | solution.py:228
  11.2 0.0 collective-permute-done.x_parts
  11.2 1.1 %collective-permute-done.1.y_parts = f32[120,128]{1,0:T(8,128)S(1)} collective-permute-done((f32[120,128]{1,0:T(8,128)S(1)}, f32[120,128]{1,0:T(8,128)S(1)}, u32[]{:S(2)}, u32[]{:S(2)}) %collective-permute-start.1) | collective-permute-done | bytes 61472 | tf_op jit(solution)/shard_map/ppermute | solution.py:512
  12.4 0.1 collective-permute-done.2.d_parts
  12.4 0.2 solve.1.refs_0_
  12.7 1.6 %collective-permute-start.3 = (f32[8,2048]{1,0:T(8,128)S(1)}, f32[8,2048]{1,0:T(8,128)S(1)}, u32[]{:S(2)}, u32[]{:S(2)}) collective-permute-start(f32[8,2048]{1,0:T(8,128)S(1)} %solve.1.refs_0_), channel_id=1, source_target_pairs={{0,1},{1,0},{2,3},{3,2},{4,5},{5,4},{6,7},{7,6},{8,9},{9,8},{10,11... | collective-permute-start | bytes 196616 | tf_op jit(solution)/shard_map/ppermute | solution.py:533
  14.3 2.6 %others_products.2 = (f32[448,1024]{1,0:T(8,128)S(1)}, f32[16,1024]{1,0:T(8,128)S(1)}, f32[64,192]{1,0:T(8,128)S(1)}, f32[64,192]{1,0:T(8,128)S(1)}) custom-call(f32[8,2048]{1,0:T(8,128)S(1)} %solve.1.refs_0_, bf16[64,4096]{1,0:T(8,128)(2,1)S(1)} %get-tuple-element.20.refs_4_.refs_1_, bf16[64,4096]{1,0:T(8,128)(2,1)S(1)} %get-tuple-element.22.refs_2_, ...), custom_call_target="tpu_custom_call" | custom-call | flops 1879048192 | bytes 4194304 | tf_op jit(solution)/shard_map/others_products/pallas_call | solution.py:344
  17.0 0.1 collective-permute-done.3.refs_1_.refs_0_
  17.0 2.6 %others_products.3 = (f32[448,1024]{1,0:T(8,128)S(1)}, f32[16,1024]{1,0:T(8,128)S(1)}, f32[64,192]{1,0:T(8,128)S(1)}, f32[64,192]{1,0:T(8,128)S(1)}) custom-call(f32[8,2048]{1,0:T(8,128)S(1)} %collective-permute-done.3.refs_1_.refs_0_, bf16[64,4096]{1,0:T(8,128)(2,1)S(1)} %get-tuple-element.20.refs_4_.refs_1_, ...), custom_call_target="tpu_custom_call" | custom-call | flops 1879048192 | bytes 4194304 | tf_op jit(solution)/shard_map/others_products/pallas_call | solution.py:344
  19.6 0.1 collective-permute-start.6
  19.7 0.5 %collective-permute-start.4 = (f32[16,1024]{1,0:T(8,128)S(1)}, f32[16,1024]{1,0:T(8,128)S(1)}, u32[]{:S(2)}, u32[]{:S(2)}) collective-permute-start(f32[16,1024]{1,0:T(8,128)S(1)} %get-tuple-element.27.refs_6_), channel_id=1, source_target_pairs={{0,4},{4,0},{1,5},{5,1},{2,6},{6,2},{3,7},{7,3},{8,12},{12,8},{9,1... | collective-permute-start | bytes 196616 | tf_op jit(solution)/shard_map/ppermute | solution.py:547
  20.2 0.1 collective-permute-start.5
  20.3 3.6 %own_products.1 = (f32[448,768]{1,0:T(8,128)S(1)}, f32[7,4096]{1,0:T(8,128)}) custom-call(f32[8,2048]{1,0:T(8,128)S(1)} %solve.1.refs_0_, f32[8,2048]{1,0:T(8,128)S(1)} %collective-permute-done.3.refs_1_.refs_0_, bf16[2048,1024]{1,0:T(8,128)(2,1)S(1)} %get-tuple-element.18.refs_2_.refs_3_, bf16[2048,1024]{1,0:T(8,128)(2,1)S(1)} %get-tuple-element.19.refs_3_, ...), custom_call_target="tpu_custom_call" | custom-call | flops 2818572288 | bytes 6291456 | tf_op jit(solution)/shard_map/own_products/pallas_call | solution.py:407
  23.9 0.0 collective-permute-done.5.refs_9_
  23.9 0.0 collective-permute-done.4.refs_7_
  23.9 0.0 collective-permute-done.6.refs_10_
  23.9 2.7 %finish.1 = f32[448,1024]{1,0:T(8,128)} custom-call(f32[8,2048]{1,0:T(8,128)S(1)} %solve.1.refs_0_, f32[8,2048]{1,0:T(8,128)S(1)} %collective-permute-done.3.refs_1_.refs_0_, bf16[2048,1024]{1,0:T(8,128)(2,1)S(1)} %get-tuple-element.18.refs_2_.refs_3_, bf16[2048,1024]{1,0:T(8,128)(2,1)S(1)} %get-tuple-element.19.refs_3_, ...), custom_call_target="tpu_custom_call" | custom-call | tf_op jit(solution)/shard_map/finish/pallas_call | solution.py:493
Async XLA Ops:
  3.8 7.5 %collective-permute-start = (f32[120,128]{1,0:T(8,128)S(1)}, f32[120,128]{1,0:T(8,128)S(1)}, u32[]{:S(2)}, u32[]{:S(2)}) collective-permute-start(f32[120,128]{1,0:T(8,128)S(1)} %get-tuple-element.17.own_parts), channel_id=1, source_target_pairs={{0,16},{8,24},{16,0},{24,8},{1,17},{9,25},{17,1},{25,9},{2,18},{10... | collective-permute-start | bytes 184328 | tf_op jit(solution)/shard_map/ppermute | solution.py:512
  6.8 5.6 %collective-permute-start.1 = (f32[120,128]{1,0:T(8,128)S(1)}, f32[120,128]{1,0:T(8,128)S(1)}, u32[]{:S(2)}, u32[]{:S(2)}) collective-permute-start(f32[120,128]{1,0:T(8,128)S(1)} %get-tuple-element.17.own_parts), channel_id=1, source_target_pairs={{0,24},{8,16},{16,8},{24,0},{1,25},{9,17},{17,9},{25,1},{2,26},{10... | collective-permute-start | bytes 184328 | tf_op jit(solution)/shard_map/ppermute | solution.py:512
  8.2 4.2 %collective-permute-start.2 = (f32[120,128]{1,0:T(8,128)S(1)}, f32[120,128]{1,0:T(8,128)S(1)}, u32[]{:S(2)}, u32[]{:S(2)}) collective-permute-start(f32[120,128]{1,0:T(8,128)S(1)} %get-tuple-element.17.own_parts), channel_id=1, source_target_pairs={{0,8},{8,0},{16,24},{24,16},{1,9},{9,1},{17,25},{25,17},{2,10},{10... | collective-permute-start | bytes 184328 | tf_op jit(solution)/shard_map/ppermute | solution.py:512
  12.7 4.3 %collective-permute-start.3 = (f32[8,2048]{1,0:T(8,128)S(1)}, f32[8,2048]{1,0:T(8,128)S(1)}, u32[]{:S(2)}, u32[]{:S(2)}) collective-permute-start(f32[8,2048]{1,0:T(8,128)S(1)} %solve.1.refs_0_), channel_id=1, source_target_pairs={{0,1},{1,0},{2,3},{3,2},{4,5},{5,4},{6,7},{7,6},{8,9},{9,8},{10,11... | collective-permute-start | bytes 196616 | tf_op jit(solution)/shard_map/ppermute | solution.py:533
  19.6 4.3 %collective-permute-start.6 = (f32[448,1024]{1,0:T(8,128)S(1)}, f32[448,1024]{1,0:T(8,128)S(1)}, u32[]{:S(2)}, u32[]{:S(2)}) collective-permute-start(f32[448,1024]{1,0:T(8,128)S(1)} %get-tuple-element.30), channel_id=1, source_target_pairs={{0,4},{4,0},{1,5},{5,1},{2,6},{6,2},{3,7},{7,3},{8,12},{12,8},{9,1... | collective-permute-start | bytes 5505032 | tf_op jit(solution)/shard_map/ppermute | solution.py:549
  19.7 4.2 %collective-permute-start.4 = (f32[16,1024]{1,0:T(8,128)S(1)}, f32[16,1024]{1,0:T(8,128)S(1)}, u32[]{:S(2)}, u32[]{:S(2)}) collective-permute-start(f32[16,1024]{1,0:T(8,128)S(1)} %get-tuple-element.27.refs_6_), channel_id=1, source_target_pairs={{0,4},{4,0},{1,5},{5,1},{2,6},{6,2},{3,7},{7,3},{8,12},{12,8},{9,1... | collective-permute-start | bytes 196616 | tf_op jit(solution)/shard_map/ppermute | solution.py:547
  20.2 3.7 %collective-permute-start.5 = (f32[64,192]{1,0:T(8,128)S(1)}, f32[64,192]{1,0:T(8,128)S(1)}, u32[]{:S(2)}, u32[]{:S(2)}) collective-permute-start(f32[64,192]{1,0:T(8,128)S(1)} %get-tuple-element.29), channel_id=1, source_target_pairs={{0,4},{4,0},{1,5},{5,1},{2,6},{6,2},{3,7},{7,3},{8,12},{12,8},{9,1... | collective-permute-start | bytes 147464 | tf_op jit(solution)/shard_map/ppermute | solution.py:548

commit v4 on v3

--- a/solution.py
+++ b/solution.py
@@ -308,13 +308,15 @@
         rounded = [pieces[0][k : k + 1] for k in range(types)]
         design_rows(left, others, rounded, cols, others.shape[0])
         left[n_rows:, :] = stacked(pieces, 32)
-        w_parts = split3(jnp.concatenate([r * p for r in rounded], axis=0))
-        for s in range(3):
-            weights[s * 64 : s * 64 + 64, :] = stacked([w_parts[s]], 64)
+        w = jnp.concatenate([r * p for r in rounded], axis=0)
+        high = w.astype(BF16).astype(F32)
+        weights[:64, :] = stacked([high], 64)
+        weights[64:, :] = stacked([w - high], 64)
         out = jnp.dot(left[...], held[here, :], preferred_element_type=F32)
         contract = (((1,), (1,)), ((), ()))
-        co = lax.dot_general(others[:, cols], weights[...], contract, preferred_element_type=F32)
-        cm = lax.dot_general(mine[:, cols], weights[...], contract, preferred_element_type=F32)
+        both = jnp.concatenate([others[:, cols], mine[:, cols]], axis=0)
+        both = lax.dot_general(both, weights[...], contract, preferred_element_type=F32)
+        co, cm = both[: others.shape[0]], both[others.shape[0] :]
         py = out[n_rows : n_rows + ROWS] + (
             out[n_rows + ROWS : n_rows + 2 * ROWS] + out[n_rows + 2 * ROWS : n_rows + 3 * ROWS]
         )
@@ -348,12 +350,12 @@
         out_shape=[
             jax.ShapeDtypeStruct((types * n_others, genes), F32),
             jax.ShapeDtypeStruct((2 * ROWS, genes), F32),
-            jax.ShapeDtypeStruct((n_mine, 192), F32),
-            jax.ShapeDtypeStruct((n_others, 192), F32),
+            jax.ShapeDtypeStruct((n_mine, 128), F32),
+            jax.ShapeDtypeStruct((n_others, 128), F32),
         ],
         scratch_shapes=[
             pltpu.VMEM((types * n_others + 32, step), BF16),
-            pltpu.VMEM((192, step), BF16),
+            pltpu.VMEM((128, step), BF16),
         ],
         compiler_params=pltpu.CompilerParams(vmem_limit_bytes=VMEM_LIMIT),
         cost_estimate=pl.CostEstimate(
@@ -365,29 +367,19 @@
     )(p, mine, others, held, *before)
 
 
-def own_dot(types, step, p_in, mine, held, lanes, left, add):
-    first_col = 0
-    first = True
-    for p_ref, held_ref in zip(p_in, held):
-        samples = held_ref.shape[0]
-        for c in range(samples // step):
-            here = slice(c * step, (c + 1) * step)
-            cols = slice(first_col + c * step, first_col + (c + 1) * step)
-            rounded = p_ref[:, here].astype(BF16).astype(F32)
-            design_rows(left, mine, [rounded[k : k + 1] for k in range(types)], cols, mine.shape[0])
-            add(jnp.dot(left[...], held_ref[here, lanes], preferred_element_type=F32), first)
-            first = False
-        first_col += samples
+def own_dot(types, step, first_col, p_ref, mine, held, lanes, left, add):
+    for c in range(held.shape[0] // step):
+        here = slice(c * step, (c + 1) * step)
+        cols = slice(first_col + c * step, first_col + (c + 1) * step)
+        rounded = p_ref[:, here].astype(BF16).astype(F32)
+        design_rows(left, mine, [rounded[k : k + 1] for k in range(types)], cols, mine.shape[0])
+        add(jnp.dot(left[...], held[here, lanes], preferred_element_type=F32), first_col + c == 0)
 
 
 def own_kernel(types, step, halves, *refs):
     p_in, held, mine = refs[:halves], refs[halves : 2 * halves], refs[2 * halves]
-    cross, props, left = refs[2 * halves + 1 :]
+    cross, left = refs[2 * halves + 1 :]
     half = p_in[0].shape[1]
-    side = lax.rem(lax.axis_index("variant"), halves)
-    for i in range(halves):
-        at = pl.multiple_of(lax.rem(side + i, halves) * half, half)
-        props[:, pl.ds(at, half)] = p_in[i][:types, :]
 
     def add(out, first):
         if first:
@@ -395,7 +387,9 @@
         else:
             cross[...] += out
 
-    own_dot(types, step, p_in, mine, held, slice(0, cross.shape[1]), left, add)
+    lanes = slice(0, cross.shape[1])
+    for i in range(halves):
+        own_dot(types, step, i * half, p_in[i], mine, held[i], lanes, left, add)
 
 
 def own_products(p, mine, held, columns, types):
@@ -407,11 +401,8 @@
     return pl.pallas_call(
         functools.partial(own_kernel, types, step, halves),
         in_specs=[vmem] * (2 * halves + 1),
-        out_specs=[vmem] * 2,
-        out_shape=[
-            jax.ShapeDtypeStruct((rows, columns), F32),
-            jax.ShapeDtypeStruct((types, samples), F32),
-        ],
+        out_specs=vmem,
+        out_shape=jax.ShapeDtypeStruct((rows, columns), F32),
         scratch_shapes=[pltpu.VMEM((rows, step), BF16)],
         compiler_params=pltpu.CompilerParams(vmem_limit_bytes=VMEM_LIMIT),
         cost_estimate=pl.CostEstimate(
@@ -426,16 +417,35 @@
     before = refs[2 * halves + 1]
     refs = refs[2 * halves + 2 :]
     smalls, corrs, blocks = refs[: 1 + peers], refs[1 + peers : 2 + 2 * peers], refs[2 + 2 * peers : 2 + 3 * peers]
-    out, left, turned, last, ready, sems = refs[2 + 3 * peers :]
+    out, props_out, left, turned, last, ready, sems, props, props_sems = refs[2 + 3 * peers :]
     n_mine = mine.shape[0]
     genes, columns = held[0].shape[1], before.shape[1]
+
+    half = p_in[0].shape[1]
+    side = lax.rem(lax.axis_index("variant"), halves)
+    copies = []
+    for i in range(halves):
+        at = pl.multiple_of(lax.rem(side + i, halves) * half, half)
+        props[i] = p_in[i][:types, :]
+        copy = pltpu.make_async_copy(props.at[i], props_out.at[:, pl.ds(at, half)], props_sems.at[i])
+        copy.start()
+        copies.append(copy)
+    lanes = slice(columns, genes)
+
+    def add(out, first):
+        if first:
+            last[...] = out
+        else:
+            last[...] += out
+
+    own_dot(types, step, 0, p_in[0], mine, held[0], lanes, left, add)
 
     small = smalls[0][...]
     corr = corrs[0][...]
     for i in range(peers):
         small = small + smalls[1 + i][...]
         corr = corr + corrs[1 + i][...]
-    corr = corr[:, 0:64] + (corr[:, 64:128] + corr[:, 128:192])
+    corr = corr[:, 0:64] + corr[:, 64:128]
     corr_t = corr.T
     low, inv = cholesky(entries(small[ROWS:, :LANES]), types)
     like = (1, genes)
@@ -451,34 +461,27 @@
             [c[0], c[0], c[0], c[1], c[1], c[2]], axis=0
         )
     turned_b = turned[...].astype(BF16)
-    copies = []
 
     def write(source, begin, end):
         fitted = lax.dot_general(
             turned_b, right[:, begin:end], (((0,), (0,)), ((), ())), preferred_element_type=F32
         )
         for t in range(begin // LANES, end // LANES):
-            lanes = slice(t * LANES, (t + 1) * LANES)
+            tile = slice(t * LANES, (t + 1) * LANES)
             here = slice(t * LANES - begin, (t + 1) * LANES - begin)
             for k in range(types):
                 rows = slice(k * n_mine, k * n_mine + own)
                 value = source[rows, here] - fitted[rows, here]
                 for block in blocks:
-                    value = value + block[k * own : (k + 1) * own, lanes]
+                    value = value + block[k * own : (k + 1) * own, tile]
                 ready[t, pl.ds(k, own, stride=types), :] = value * scale
             copy = pltpu.make_async_copy(ready.at[t], out.at[:, pl.ds(t * LANES, LANES)], sems.at[t])
             copy.start()
             copies.append(copy)
 
     write(before, 0, columns)
-
-    def add(out, first):
-        if first:
-            last[...] = out
-        else:
-            last[...] += out
-
-    own_dot(types, step, p_in, mine, held, slice(columns, genes), left, add)
+    for i in range(1, halves):
+        own_dot(types, step, i * half, p_in[i], mine, held[i], lanes, left, add)
     write(last, columns, genes)
     for copy in copies:
         copy.wait()
@@ -493,14 +496,19 @@
     return pl.pallas_call(
         functools.partial(finish_kernel, types, step, scale, own, halves, len(blocks)),
         in_specs=[vmem] * (2 * halves + 2 + 2 * len(smalls) + len(blocks)),
-        out_specs=pl.BlockSpec(memory_space=pl.ANY),
-        out_shape=jax.ShapeDtypeStruct((types * own, genes), F32),
+        out_specs=[pl.BlockSpec(memory_space=pl.ANY)] * 2,
+        out_shape=[
+            jax.ShapeDtypeStruct((types * own, genes), F32),
+            jax.ShapeDtypeStruct((types, halves * p[0].shape[1]), F32),
+        ],
         scratch_shapes=[
             pltpu.VMEM((rows, step), BF16),
             pltpu.VMEM((48, rows), F32),
             pltpu.VMEM((rows, genes - columns), F32),
             pltpu.VMEM((genes // LANES, types * own, LANES), F32),
             pltpu.SemaphoreType.DMA((genes // LANES,)),
+            pltpu.VMEM((halves, types, p[0].shape[1]), F32),
+            pltpu.SemaphoreType.DMA((halves,)),
         ],
         compiler_params=pltpu.CompilerParams(vmem_limit_bytes=VMEM_LIMIT),
         name="finish",
@@ -548,8 +556,8 @@
         corrs.append(lax.ppermute(corr, "sample", pairs))
         blocks.append(lax.ppermute(cross, "sample", pairs))
     columns = g_dev * 3 // 4 // LANES * LANES
-    before, props_t = own_products(solved, mine, held, columns, types)
-    interaction = finish(
+    before = own_products(solved, mine, held, columns, types)
+    interaction, props_t = finish(
         solved, mine, held, before, smalls, corrs, blocks, own, types, scale
     )
     return interaction, props_t.T

time: 26.9 us -> 26 us (0.967)
  Pallas kernels: 17.9 us -> 16.4 us
  waiting for transfers between devices: 1.28 us -> 1.86 us
    pallas_call x1, Pallas kernels: 3.62 us -> 3.02 us  [own_products(): pl.pallas_call(functools.partial(own_kernel, types, step, halves), in_spe...]
    pallas_call x2, Pallas kernels: 5.27 us -> 4.69 us  [others_products(): pl.pallas_call(functools.partial(others_kernel, types, step, first_col, b...]
    ppermute x1, waiting for transfers between devices: 0.01 us -> 0.3 us  [local(): corrs.append(lax.ppermute(corr, 'sample', pairs))]
    pallas_call x1, Pallas kernels: 2.75 us -> 2.46 us  [finish(): pl.pallas_call(functools.partial(finish_kernel, types, step, scale, own,...]
    ppermute x1, waiting for transfers between devices: 0.06 us -> 0.34 us  [local(): solved.append(lax.ppermute(solved[0], 'variant', pairs))]
  transfers between devices with their start and end apart: 7 -> 7, of which waited for: 3 -> 4; matrix products, arithmetic and copies ran while one was open for 0% -> 0% of each run, Pallas kernels for 34% -> 32%
where the time goes in v4:
time: 26 us; the launch traced here: 25.8 us
  Pallas kernels  16.4 us (63%)
  starting transfers between devices  6.86 us (26%)
  waiting for transfers between devices  1.86 us (7%)
  between operations  0.69 us (3%)
    pallas_call x2, Pallas kernels, others_products(): pl.pallas_call(functools.partial(others_kernel, types, step, first_col, b...  4.69 us
    ppermute x3, starting transfers between devices, swap(): return lax.ppermute(part, 'gene', [(i, i ^ offset) for i in range(n_gene)])  4.57 us
    pallas_call x1, Pallas kernels, right_sides(): pl.pallas_call(functools.partial(rhs_kernel, types, halves, pieces), in_s...  3.12 us
    pallas_call x1, Pallas kernels, own_products(): pl.pallas_call(functools.partial(own_kernel, types, step, halves), in_spe...  3.02 us
    pallas_call x1, Pallas kernels, prepare(): pl.pallas_call(functools.partial(prepare_kernel, own, halves, pieces), in...  2.88 us
    pallas_call x1, Pallas kernels, finish(): pl.pallas_call(functools.partial(finish_kernel, types, step, scale, own,...  2.46 us
    ppermute x1, starting transfers between devices, local(): solved.append(lax.ppermute(solved[0], 'variant', pairs))  1.64 us
    ppermute x3, waiting for transfers between devices, swap(): return lax.ppermute(part, 'gene', [(i, i ^ offset) for i in range(n_gene)])  1.21 us
  transfers between devices with their start and end apart: 7, of which 4 were waited for; matrix products, arithmetic and copies ran while one was open for 0% of the time, Pallas kernels for 32%

profile of v4, /device:TPU:0, one launch (start us, length us, event | category | flops | bytes accessed | tf_op | source)
XLA Modules:
  0.0 25.8 jit_solution(18404614498335113707)
XLA Ops:
  0.6 3.1 %right_sides.1 = (bf16[2048,1024]{1,0:T(8,128)(2,1)S(1)}, f32[120,128]{1,0:T(8,128)S(1)}) custom-call(s32[500]{0:T(512)} %signature_in.1, f32[7,1024]{1,0:T(8,128)} %bitcast.2, bf16[4096,1024]{1,0:T(8,128)(2,1)} %expression.3), custom_call_target="tpu_custom_call" | custom-call | flops 134217728 | bytes 4194304 | tf_op jit(solution)/shard_map/right_sides/pallas_call | solution.py:169
  3.8 3.0 %collective-permute-start = (f32[120,128]{1,0:T(8,128)S(1)}, f32[120,128]{1,0:T(8,128)S(1)}, u32[]{:S(2)}, u32[]{:S(2)}) collective-permute-start(f32[120,128]{1,0:T(8,128)S(1)} %get-tuple-element.17.own_parts), channel_id=1, source_target_pairs={{0,16},{8,24},{16,0},{24,8},{1,17},{9,25},{17,1},{25,9},{2,18},{10... | collective-permute-start | bytes 184328 | tf_op jit(solution)/shard_map/ppermute | solution.py:520
  6.8 1.4 %collective-permute-start.1 = (f32[120,128]{1,0:T(8,128)S(1)}, f32[120,128]{1,0:T(8,128)S(1)}, u32[]{:S(2)}, u32[]{:S(2)}) collective-permute-start(f32[120,128]{1,0:T(8,128)S(1)} %get-tuple-element.17.own_parts), channel_id=1, source_target_pairs={{0,24},{8,16},{16,8},{24,0},{1,25},{9,17},{17,9},{25,1},{2,26},{10... | collective-permute-start | bytes 184328 | tf_op jit(solution)/shard_map/ppermute | solution.py:520
  8.2 0.1 collective-permute-start.2
  8.3 2.9 %prepare.1 = (bf16[64,4096]{1,0:T(8,128)(2,1)S(1)}, bf16[64,4096]{1,0:T(8,128)(2,1)S(1)}, bf16[2048,1024]{1,0:T(8,128)(2,1)S(1)}) custom-call(s32[4096,128]{1,0:T(8,128)} %dosage_in.1, bf16[4096,1024]{1,0:T(8,128)(2,1)} %expression.3), custom_call_target="tpu_custom_call" | custom-call | flops 524288 | bytes 3145728 | tf_op jit(solution)/shard_map/prepare/pallas_call | solution.py:228
  11.2 0.0 collective-permute-done.x_parts
  11.2 1.1 %collective-permute-done.1.y_parts = f32[120,128]{1,0:T(8,128)S(1)} collective-permute-done((f32[120,128]{1,0:T(8,128)S(1)}, f32[120,128]{1,0:T(8,128)S(1)}, u32[]{:S(2)}, u32[]{:S(2)}) %collective-permute-start.1) | collective-permute-done | bytes 61472 | tf_op jit(solution)/shard_map/ppermute | solution.py:520
  12.4 0.1 collective-permute-done.2.d_parts
  12.4 0.2 solve.1.refs_0_
  12.7 1.6 %collective-permute-start.3 = (f32[8,2048]{1,0:T(8,128)S(1)}, f32[8,2048]{1,0:T(8,128)S(1)}, u32[]{:S(2)}, u32[]{:S(2)}) collective-permute-start(f32[8,2048]{1,0:T(8,128)S(1)} %solve.1.refs_0_), channel_id=1, source_target_pairs={{0,1},{1,0},{2,3},{3,2},{4,5},{5,4},{6,7},{7,6},{8,9},{9,8},{10,11... | collective-permute-start | bytes 196616 | tf_op jit(solution)/shard_map/ppermute | solution.py:541
  14.3 2.3 %others_products.2 = (f32[448,1024]{1,0:T(8,128)S(1)}, f32[16,1024]{1,0:T(8,128)S(1)}, f32[64,128]{1,0:T(8,128)S(1)}, f32[64,128]{1,0:T(8,128)S(1)}) custom-call(f32[8,2048]{1,0:T(8,128)S(1)} %solve.1.refs_0_, bf16[64,4096]{1,0:T(8,128)(2,1)S(1)} %get-tuple-element.20.refs_4_.refs_1_, bf16[64,4096]{1,0:T(8,128)(2,1)S(1)} %get-tuple-element.21.refs_2_, ...), custom_call_target="tpu_custom_call" | custom-call | flops 1879048192 | bytes 4194304 | tf_op jit(solution)/shard_map/others_products/pallas_call | solution.py:346
  16.7 0.3 %collective-permute-done.3.refs_1_.refs_0_ = f32[8,2048]{1,0:T(8,128)S(1)} collective-permute-done((f32[8,2048]{1,0:T(8,128)S(1)}, f32[8,2048]{1,0:T(8,128)S(1)}, u32[]{:S(2)}, u32[]{:S(2)}) %collective-permute-start.3) | collective-permute-done | bytes 65568 | tf_op jit(solution)/shard_map/ppermute | solution.py:541
  17.0 2.3 %others_products.3 = (f32[448,1024]{1,0:T(8,128)S(1)}, f32[16,1024]{1,0:T(8,128)S(1)}, f32[64,128]{1,0:T(8,128)S(1)}, f32[64,128]{1,0:T(8,128)S(1)}) custom-call(f32[8,2048]{1,0:T(8,128)S(1)} %collective-permute-done.3.refs_1_.refs_0_, bf16[64,4096]{1,0:T(8,128)(2,1)S(1)} %get-tuple-element.20.refs_4_.refs_1_, ...), custom_call_target="tpu_custom_call" | custom-call | flops 1879048192 | bytes 4194304 | tf_op jit(solution)/shard_map/others_products/pallas_call | solution.py:346
  19.4 0.1 collective-permute-start.6
  19.4 0.5 %collective-permute-start.4 = (f32[16,1024]{1,0:T(8,128)S(1)}, f32[16,1024]{1,0:T(8,128)S(1)}, u32[]{:S(2)}, u32[]{:S(2)}) collective-permute-start(f32[16,1024]{1,0:T(8,128)S(1)} %get-tuple-element.26.refs_6_), channel_id=1, source_target_pairs={{0,4},{4,0},{1,5},{5,1},{2,6},{6,2},{3,7},{7,3},{8,12},{12,8},{9,1... | collective-permute-start | bytes 196616 | tf_op jit(solution)/shard_map/ppermute | solution.py:555
  19.9 0.1 collective-permute-start.5
  20.0 3.0 %own_products.1.refs_5_ = f32[448,768]{1,0:T(8,128)S(1)} custom-call(f32[8,2048]{1,0:T(8,128)S(1)} %solve.1.refs_0_, f32[8,2048]{1,0:T(8,128)S(1)} %collective-permute-done.3.refs_1_.refs_0_, bf16[2048,1024]{1,0:T(8,128)(2,1)S(1)} %get-tuple-element.18.refs_2_.refs_3_, bf16[2048,1024]{1,0:T(8,128)(2,1)S(1)} %get-tuple-element.19.refs_3_, ...), custom_call_target="tpu_custom_call" | custom-call | flops 2818572288 | bytes 6291456 | tf_op jit(solution)/shard_map/own_products/pallas_call | solution.py:401
  23.1 0.3 %collective-permute-done.5.refs_9_ = f32[64,128]{1,0:T(8,128)S(1)} collective-permute-done((f32[64,128]{1,0:T(8,128)S(1)}, f32[64,128]{1,0:T(8,128)S(1)}, u32[]{:S(2)}, u32[]{:S(2)}) %collective-permute-start.5) | collective-permute-done | bytes 32800 | tf_op jit(solution)/shard_map/ppermute | solution.py:556
  23.4 0.0 collective-permute-done.4.refs_7_
  23.4 0.0 collective-permute-done.6.refs_10_
  23.4 2.5 %finish.1 = (f32[448,1024]{1,0:T(8,128)}, f32[7,4096]{1,0:T(8,128)}) custom-call(f32[8,2048]{1,0:T(8,128)S(1)} %solve.1.refs_0_, f32[8,2048]{1,0:T(8,128)S(1)} %collective-permute-done.3.refs_1_.refs_0_, bf16[2048,1024]{1,0:T(8,128)(2,1)S(1)} %get-tuple-element.18.refs_2_.refs_3_, bf16[2048,1024]{1,0:T(8,128)(2,1)S(1)} %get-tuple-element.19.refs_3_, ...), custom_call_target="tpu_custom_call" | custom-call | tf_op jit(solution)/shard_map/finish/pallas_call | solution.py:496
Async XLA Ops:
  3.8 7.5 %collective-permute-start = (f32[120,128]{1,0:T(8,128)S(1)}, f32[120,128]{1,0:T(8,128)S(1)}, u32[]{:S(2)}, u32[]{:S(2)}) collective-permute-start(f32[120,128]{1,0:T(8,128)S(1)} %get-tuple-element.17.own_parts), channel_id=1, source_target_pairs={{0,16},{8,24},{16,0},{24,8},{1,17},{9,25},{17,1},{25,9},{2,18},{10... | collective-permute-start | bytes 184328 | tf_op jit(solution)/shard_map/ppermute | solution.py:520
  6.8 5.6 %collective-permute-start.1 = (f32[120,128]{1,0:T(8,128)S(1)}, f32[120,128]{1,0:T(8,128)S(1)}, u32[]{:S(2)}, u32[]{:S(2)}) collective-permute-start(f32[120,128]{1,0:T(8,128)S(1)} %get-tuple-element.17.own_parts), channel_id=1, source_target_pairs={{0,24},{8,16},{16,8},{24,0},{1,25},{9,17},{17,9},{25,1},{2,26},{10... | collective-permute-start | bytes 184328 | tf_op jit(solution)/shard_map/ppermute | solution.py:520
  8.2 4.2 %collective-permute-start.2 = (f32[120,128]{1,0:T(8,128)S(1)}, f32[120,128]{1,0:T(8,128)S(1)}, u32[]{:S(2)}, u32[]{:S(2)}) collective-permute-start(f32[120,128]{1,0:T(8,128)S(1)} %get-tuple-element.17.own_parts), channel_id=1, source_target_pairs={{0,8},{8,0},{16,24},{24,16},{1,9},{9,1},{17,25},{25,17},{2,10},{10... | collective-permute-start | bytes 184328 | tf_op jit(solution)/shard_map/ppermute | solution.py:520
  12.7 4.3 %collective-permute-start.3 = (f32[8,2048]{1,0:T(8,128)S(1)}, f32[8,2048]{1,0:T(8,128)S(1)}, u32[]{:S(2)}, u32[]{:S(2)}) collective-permute-start(f32[8,2048]{1,0:T(8,128)S(1)} %solve.1.refs_0_), channel_id=1, source_target_pairs={{0,1},{1,0},{2,3},{3,2},{4,5},{5,4},{6,7},{7,6},{8,9},{9,8},{10,11... | collective-permute-start | bytes 196616 | tf_op jit(solution)/shard_map/ppermute | solution.py:541
  19.4 4.0 %collective-permute-start.6 = (f32[448,1024]{1,0:T(8,128)S(1)}, f32[448,1024]{1,0:T(8,128)S(1)}, u32[]{:S(2)}, u32[]{:S(2)}) collective-permute-start(f32[448,1024]{1,0:T(8,128)S(1)} %get-tuple-element.29), channel_id=1, source_target_pairs={{0,4},{4,0},{1,5},{5,1},{2,6},{6,2},{3,7},{7,3},{8,12},{12,8},{9,1... | collective-permute-start | bytes 5505032 | tf_op jit(solution)/shard_map/ppermute | solution.py:557
  19.4 3.9 %collective-permute-start.4 = (f32[16,1024]{1,0:T(8,128)S(1)}, f32[16,1024]{1,0:T(8,128)S(1)}, u32[]{:S(2)}, u32[]{:S(2)}) collective-permute-start(f32[16,1024]{1,0:T(8,128)S(1)} %get-tuple-element.26.refs_6_), channel_id=1, source_target_pairs={{0,4},{4,0},{1,5},{5,1},{2,6},{6,2},{3,7},{7,3},{8,12},{12,8},{9,1... | collective-permute-start | bytes 196616 | tf_op jit(solution)/shard_map/ppermute | solution.py:555
  19.9 3.4 %collective-permute-start.5 = (f32[64,128]{1,0:T(8,128)S(1)}, f32[64,128]{1,0:T(8,128)S(1)}, u32[]{:S(2)}, u32[]{:S(2)}) collective-permute-start(f32[64,128]{1,0:T(8,128)S(1)} %get-tuple-element.28), channel_id=1, source_target_pairs={{0,4},{4,0},{1,5},{5,1},{2,6},{6,2},{3,7},{7,3},{8,12},{12,8},{9,1... | collective-permute-start | bytes 98312 | tf_op jit(solution)/shard_map/ppermute | solution.py:556

commit v5 on v4

--- a/solution.py
+++ b/solution.py
@@ -367,42 +367,52 @@
     )(p, mine, others, held, *before)
 
 
-def own_dot(types, step, first_col, p_ref, mine, held, lanes, left, add):
-    for c in range(held.shape[0] // step):
+def own_dot(types, step, first_col, p_ref, mine, held, lanes, left, add, beside=None):
+    count = held.shape[0] // step
+    for c in range(count):
         here = slice(c * step, (c + 1) * step)
         cols = slice(first_col + c * step, first_col + (c + 1) * step)
         rounded = p_ref[:, here].astype(BF16).astype(F32)
         design_rows(left, mine, [rounded[k : k + 1] for k in range(types)], cols, mine.shape[0])
+        if beside is not None:
+            beside(c, count)
         add(jnp.dot(left[...], held[here, lanes], preferred_element_type=F32), first_col + c == 0)
 
 
 def own_kernel(types, step, halves, *refs):
     p_in, held, mine = refs[:halves], refs[halves : 2 * halves], refs[2 * halves]
-    cross, left = refs[2 * halves + 1 :]
+    cross, tail, left = refs[2 * halves + 1 :]
     half = p_in[0].shape[1]
 
-    def add(out, first):
-        if first:
-            cross[...] = out
-        else:
-            cross[...] += out
-
-    lanes = slice(0, cross.shape[1])
+    def add_to(total):
+        def add(out, first):
+            if first:
+                total[...] = out
+            else:
+                total[...] += out
+
+        return add
+
+    columns, genes = cross.shape[1], held[0].shape[1]
     for i in range(halves):
-        own_dot(types, step, i * half, p_in[i], mine, held[i], lanes, left, add)
+        own_dot(types, step, i * half, p_in[i], mine, held[i], slice(0, columns), left, add_to(cross))
+    own_dot(types, step, 0, p_in[0], mine, held[0], slice(columns, genes), left, add_to(tail))
 
 
 def own_products(p, mine, held, columns, types):
     halves = len(p)
-    samples = halves * p[0].shape[1]
+    samples, genes = halves * p[0].shape[1], held[0].shape[1]
     step = 512
     rows = types * mine.shape[0]
     vmem = pl.BlockSpec(memory_space=pltpu.VMEM)
     return pl.pallas_call(
         functools.partial(own_kernel, types, step, halves),
         in_specs=[vmem] * (2 * halves + 1),
-        out_specs=vmem,
-        out_shape=jax.ShapeDtypeStruct((rows, columns), F32),
+        out_specs=[vmem] * 2,
+        out_shape=[
+            jax.ShapeDtypeStruct((rows, columns), F32),
+            jax.ShapeDtypeStruct((rows, genes - columns), F32),
+        ],
         scratch_shapes=[pltpu.VMEM((rows, step), BF16)],
         compiler_params=pltpu.CompilerParams(vmem_limit_bytes=VMEM_LIMIT),
         cost_estimate=pl.CostEstimate(
@@ -414,8 +424,8 @@
 
 def finish_kernel(types, step, scale, own, halves, peers, *refs):
     p_in, held, mine = refs[:halves], refs[halves : 2 * halves], refs[2 * halves]
-    before = refs[2 * halves + 1]
-    refs = refs[2 * halves + 2 :]
+    before, tail = refs[2 * halves + 1 : 2 * halves + 3]
+    refs = refs[2 * halves + 3 :]
     smalls, corrs, blocks = refs[: 1 + peers], refs[1 + peers : 2 + 2 * peers], refs[2 + 2 * peers : 2 + 3 * peers]
     out, props_out, left, turned, last, ready, sems, props, props_sems = refs[2 + 3 * peers :]
     n_mine = mine.shape[0]
@@ -432,13 +442,11 @@
         copies.append(copy)
     lanes = slice(columns, genes)
 
+    seen = [tail]
+
     def add(out, first):
-        if first:
-            last[...] = out
-        else:
-            last[...] += out
-
-    own_dot(types, step, 0, p_in[0], mine, held[0], lanes, left, add)
+        last[...] = seen[-1][...] + out
+        seen.append(last)
 
     small = smalls[0][...]
     corr = corrs[0][...]
@@ -460,34 +468,42 @@
         turned[:, k * n_mine : (k + 1) * n_mine] = jnp.concatenate(
             [c[0], c[0], c[0], c[1], c[1], c[2]], axis=0
         )
-    turned_b = turned[...].astype(BF16)
-
-    def write(source, begin, end):
-        fitted = lax.dot_general(
-            turned_b, right[:, begin:end], (((0,), (0,)), ((), ())), preferred_element_type=F32
+    turned_b = turned[...].T.astype(BF16)
+
+    def write(t):
+        tile = slice(t * LANES, (t + 1) * LANES)
+        source, here = before, tile
+        if t * LANES >= columns:
+            source, here = seen[-1], slice(t * LANES - columns, (t + 1) * LANES - columns)
+        fitted = jnp.dot(turned_b, right[:, tile], preferred_element_type=F32)
+        for k in range(types):
+            rows = slice(k * n_mine, k * n_mine + own)
+            value = source[rows, here] - fitted[rows]
+            for block in blocks:
+                value = value + block[k * own : (k + 1) * own, tile]
+            ready[t, pl.ds(k, own, stride=types), :] = value * scale
+        copy = pltpu.make_async_copy(ready.at[t], out.at[:, pl.ds(t * LANES, LANES)], sems.at[t])
+        copy.start()
+        copies.append(copy)
+
+    early, tiles = columns // LANES, genes // LANES
+
+    def beside(c, count):
+        for t in range(early * c // count, early * (c + 1) // count):
+            write(t)
+
+    for i in range(1, halves):
+        own_dot(
+            types, step, i * half, p_in[i], mine, held[i], lanes, left, add,
+            beside if i == halves - 1 else None,
         )
-        for t in range(begin // LANES, end // LANES):
-            tile = slice(t * LANES, (t + 1) * LANES)
-            here = slice(t * LANES - begin, (t + 1) * LANES - begin)
-            for k in range(types):
-                rows = slice(k * n_mine, k * n_mine + own)
-                value = source[rows, here] - fitted[rows, here]
-                for block in blocks:
-                    value = value + block[k * own : (k + 1) * own, tile]
-                ready[t, pl.ds(k, own, stride=types), :] = value * scale
-            copy = pltpu.make_async_copy(ready.at[t], out.at[:, pl.ds(t * LANES, LANES)], sems.at[t])
-            copy.start()
-            copies.append(copy)
-
-    write(before, 0, columns)
-    for i in range(1, halves):
-        own_dot(types, step, i * half, p_in[i], mine, held[i], lanes, left, add)
-    write(last, columns, genes)
+    for t in range(early if halves > 1 else 0, tiles):
+        write(t)
     for copy in copies:
         copy.wait()
 
 
-def finish(p, mine, held, before, smalls, corrs, blocks, own, types, scale):
+def finish(p, mine, held, before, tail, smalls, corrs, blocks, own, types, scale):
     halves = len(p)
     genes, columns = held[0].shape[1], before.shape[1]
     step = 512
@@ -495,7 +511,7 @@
     vmem = pl.BlockSpec(memory_space=pltpu.VMEM)
     return pl.pallas_call(
         functools.partial(finish_kernel, types, step, scale, own, halves, len(blocks)),
-        in_specs=[vmem] * (2 * halves + 2 + 2 * len(smalls) + len(blocks)),
+        in_specs=[vmem] * (2 * halves + 3 + 2 * len(smalls) + len(blocks)),
         out_specs=[pl.BlockSpec(memory_space=pl.ANY)] * 2,
         out_shape=[
             jax.ShapeDtypeStruct((types * own, genes), F32),
@@ -512,7 +528,7 @@
         ],
         compiler_params=pltpu.CompilerParams(vmem_limit_bytes=VMEM_LIMIT),
         name="finish",
-    )(*p, *held, mine, before, *smalls, *corrs, *blocks)
+    )(*p, *held, mine, before, tail, *smalls, *corrs, *blocks)
 
 
 def exchange_all(part, n_gene):
@@ -556,9 +572,9 @@
         corrs.append(lax.ppermute(corr, "sample", pairs))
         blocks.append(lax.ppermute(cross, "sample", pairs))
     columns = g_dev * 3 // 4 // LANES * LANES
-    before = own_products(solved, mine, held, columns, types)
+    before, tail = own_products(solved, mine, held, columns, types)
     interaction, props_t = finish(
-        solved, mine, held, before, smalls, corrs, blocks, own, types, scale
+        solved, mine, held, before, tail, smalls, corrs, blocks, own, types, scale
     )
     return interaction, props_t.T
 

time: 26 us -> 25.8 us (level)
  waiting for transfers between devices: 1.86 us -> 1.56 us
    pallas_call x1, Pallas kernels: 3.02 us -> 3.5 us  [own_products(): pl.pallas_call(functools.partial(own_kernel, types, step, halves), in_spe...]
    pallas_call x1, Pallas kernels: 2.46 us -> 2.1 us  [finish(): pl.pallas_call(functools.partial(finish_kernel, types, step, scale, own,...]
    ppermute x1, waiting for transfers between devices: 0.3 us -> 0.01 us  [local(): corrs.append(lax.ppermute(corr, 'sample', pairs))]
  transfers between devices with their start and end apart: 7 -> 7, of which waited for: 4 -> 3; matrix products, arithmetic and copies ran while one was open for 0% -> 0% of each run, Pallas kernels for 32% -> 34%
where the time goes in v5:
time: 25.8 us; the launch traced here: 25.7 us
  Pallas kernels  16.5 us (64%)
  starting transfers between devices  6.86 us (27%)
  waiting for transfers between devices  1.56 us (6%)
  between operations  0.71 us (3%)
    pallas_call x2, Pallas kernels, others_products(): pl.pallas_call(functools.partial(others_kernel, types, step, first_col, b...  4.69 us
    ppermute x3, starting transfers between devices, swap(): return lax.ppermute(part, 'gene', [(i, i ^ offset) for i in range(n_gene)])  4.57 us
    pallas_call x1, Pallas kernels, own_products(): pl.pallas_call(functools.partial(own_kernel, types, step, halves), in_spe...  3.5 us
    pallas_call x1, Pallas kernels, right_sides(): pl.pallas_call(functools.partial(rhs_kernel, types, halves, pieces), in_s...  3.12 us
    pallas_call x1, Pallas kernels, prepare(): pl.pallas_call(functools.partial(prepare_kernel, own, halves, pieces), in...  2.88 us
    pallas_call x1, Pallas kernels, finish(): pl.pallas_call(functools.partial(finish_kernel, types, step, scale, own,...  2.1 us
    ppermute x1, starting transfers between devices, local(): solved.append(lax.ppermute(solved[0], 'variant', pairs))  1.64 us
    ppermute x3, waiting for transfers between devices, swap(): return lax.ppermute(part, 'gene', [(i, i ^ offset) for i in range(n_gene)])  1.21 us
  transfers between devices with their start and end apart: 7, of which 3 were waited for; matrix products, arithmetic and copies ran while one was open for 0% of the time, Pallas kernels for 34%

profile of v5, /device:TPU:0, one launch (start us, length us, event | category | flops | bytes accessed | tf_op | source)
XLA Modules:
  0.0 25.7 jit_solution(17421845431206702615)
XLA Ops:
  0.6 3.1 %right_sides.1 = (bf16[2048,1024]{1,0:T(8,128)(2,1)S(1)}, f32[120,128]{1,0:T(8,128)S(1)}) custom-call(s32[500]{0:T(512)} %signature_in.1, f32[7,1024]{1,0:T(8,128)} %bitcast.2, bf16[4096,1024]{1,0:T(8,128)(2,1)} %expression.3), custom_call_target="tpu_custom_call" | custom-call | flops 134217728 | bytes 4194304 | tf_op jit(solution)/shard_map/right_sides/pallas_call | solution.py:169
  3.8 3.0 %collective-permute-start = (f32[120,128]{1,0:T(8,128)S(1)}, f32[120,128]{1,0:T(8,128)S(1)}, u32[]{:S(2)}, u32[]{:S(2)}) collective-permute-start(f32[120,128]{1,0:T(8,128)S(1)} %get-tuple-element.19.own_parts), channel_id=1, source_target_pairs={{0,16},{8,24},{16,0},{24,8},{1,17},{9,25},{17,1},{25,9},{2,18},{10... | collective-permute-start | bytes 184328 | tf_op jit(solution)/shard_map/ppermute | solution.py:536
  6.8 1.4 %collective-permute-start.1 = (f32[120,128]{1,0:T(8,128)S(1)}, f32[120,128]{1,0:T(8,128)S(1)}, u32[]{:S(2)}, u32[]{:S(2)}) collective-permute-start(f32[120,128]{1,0:T(8,128)S(1)} %get-tuple-element.19.own_parts), channel_id=1, source_target_pairs={{0,24},{8,16},{16,8},{24,0},{1,25},{9,17},{17,9},{25,1},{2,26},{10... | collective-permute-start | bytes 184328 | tf_op jit(solution)/shard_map/ppermute | solution.py:536
  8.2 0.1 collective-permute-start.2
  8.3 2.9 %prepare.1 = (bf16[64,4096]{1,0:T(8,128)(2,1)S(1)}, bf16[64,4096]{1,0:T(8,128)(2,1)S(1)}, bf16[2048,1024]{1,0:T(8,128)(2,1)S(1)}) custom-call(s32[4096,128]{1,0:T(8,128)} %dosage_in.1, bf16[4096,1024]{1,0:T(8,128)(2,1)} %expression.3), custom_call_target="tpu_custom_call" | custom-call | flops 524288 | bytes 3145728 | tf_op jit(solution)/shard_map/prepare/pallas_call | solution.py:228
  11.2 0.0 collective-permute-done.x_parts
  11.2 1.1 %collective-permute-done.1.y_parts = f32[120,128]{1,0:T(8,128)S(1)} collective-permute-done((f32[120,128]{1,0:T(8,128)S(1)}, f32[120,128]{1,0:T(8,128)S(1)}, u32[]{:S(2)}, u32[]{:S(2)}) %collective-permute-start.1) | collective-permute-done | bytes 61472 | tf_op jit(solution)/shard_map/ppermute | solution.py:536
  12.4 0.1 collective-permute-done.2.d_parts
  12.4 0.2 solve.1.refs_0_
  12.7 1.6 %collective-permute-start.3 = (f32[8,2048]{1,0:T(8,128)S(1)}, f32[8,2048]{1,0:T(8,128)S(1)}, u32[]{:S(2)}, u32[]{:S(2)}) collective-permute-start(f32[8,2048]{1,0:T(8,128)S(1)} %solve.1.refs_0_), channel_id=1, source_target_pairs={{0,1},{1,0},{2,3},{3,2},{4,5},{5,4},{6,7},{7,6},{8,9},{9,8},{10,11... | collective-permute-start | bytes 196616 | tf_op jit(solution)/shard_map/ppermute | solution.py:557
  14.3 2.3 %others_products.2 = (f32[448,1024]{1,0:T(8,128)S(1)}, f32[16,1024]{1,0:T(8,128)S(1)}, f32[64,128]{1,0:T(8,128)S(1)}, f32[64,128]{1,0:T(8,128)S(1)}) custom-call(f32[8,2048]{1,0:T(8,128)S(1)} %solve.1.refs_0_, bf16[64,4096]{1,0:T(8,128)(2,1)S(1)} %get-tuple-element.22.refs_4_.refs_1_, bf16[64,4096]{1,0:T(8,128)(2,1)S(1)} %get-tuple-element.25.refs_2_, ...), custom_call_target="tpu_custom_call" | custom-call | flops 1879048192 | bytes 4194304 | tf_op jit(solution)/shard_map/others_products/pallas_call | solution.py:346
  16.7 0.3 %collective-permute-done.3.refs_1_.refs_0_ = f32[8,2048]{1,0:T(8,128)S(1)} collective-permute-done((f32[8,2048]{1,0:T(8,128)S(1)}, f32[8,2048]{1,0:T(8,128)S(1)}, u32[]{:S(2)}, u32[]{:S(2)}) %collective-permute-start.3) | collective-permute-done | bytes 65568 | tf_op jit(solution)/shard_map/ppermute | solution.py:557
  17.0 2.3 %others_products.3 = (f32[448,1024]{1,0:T(8,128)S(1)}, f32[16,1024]{1,0:T(8,128)S(1)}, f32[64,128]{1,0:T(8,128)S(1)}, f32[64,128]{1,0:T(8,128)S(1)}) custom-call(f32[8,2048]{1,0:T(8,128)S(1)} %collective-permute-done.3.refs_1_.refs_0_, bf16[64,4096]{1,0:T(8,128)(2,1)S(1)} %get-tuple-element.22.refs_4_.refs_1_, ...), custom_call_target="tpu_custom_call" | custom-call | flops 1879048192 | bytes 4194304 | tf_op jit(solution)/shard_map/others_products/pallas_call | solution.py:346
  19.4 0.1 collective-permute-start.6
  19.4 0.5 %collective-permute-start.4 = (f32[16,1024]{1,0:T(8,128)S(1)}, f32[16,1024]{1,0:T(8,128)S(1)}, u32[]{:S(2)}, u32[]{:S(2)}) collective-permute-start(f32[16,1024]{1,0:T(8,128)S(1)} %get-tuple-element.30.refs_7_), channel_id=1, source_target_pairs={{0,4},{4,0},{1,5},{5,1},{2,6},{6,2},{3,7},{7,3},{8,12},{12,8},{9,1... | collective-permute-start | bytes 196616 | tf_op jit(solution)/shard_map/ppermute | solution.py:571
  19.9 0.1 collective-permute-start.5
  20.0 3.5 %own_products.1 = (f32[448,768]{1,0:T(8,128)S(1)}, f32[448,256]{1,0:T(8,128)S(1)}) custom-call(f32[8,2048]{1,0:T(8,128)S(1)} %solve.1.refs_0_, f32[8,2048]{1,0:T(8,128)S(1)} %collective-permute-done.3.refs_1_.refs_0_, bf16[2048,1024]{1,0:T(8,128)(2,1)S(1)} %get-tuple-element.20.refs_2_.refs_3_, bf16[2048,1024]{1,0:T(8,128)(2,1)S(1)} %get-tuple-element.21.refs_3_, ...), custom_call_target="tpu_custom_call" | custom-call | flops 2818572288 | bytes 6291456 | tf_op jit(solution)/shard_map/own_products/pallas_call | solution.py:408
  23.5 0.0 collective-permute-done.5.refs_10_
  23.5 0.0 collective-permute-done.4.refs_8_
  23.6 0.0 collective-permute-done.6.refs_11_
  23.6 2.1 %finish.1 = (f32[448,1024]{1,0:T(8,128)}, f32[7,4096]{1,0:T(8,128)}) custom-call(f32[8,2048]{1,0:T(8,128)S(1)} %solve.1.refs_0_, f32[8,2048]{1,0:T(8,128)S(1)} %collective-permute-done.3.refs_1_.refs_0_, bf16[2048,1024]{1,0:T(8,128)(2,1)S(1)} %get-tuple-element.20.refs_2_.refs_3_, bf16[2048,1024]{1,0:T(8,128)(2,1)S(1)} %get-tuple-element.21.refs_3_, ...), custom_call_target="tpu_custom_call" | custom-call | tf_op jit(solution)/shard_map/finish/pallas_call | solution.py:512
Async XLA Ops:
  3.8 7.5 %collective-permute-start = (f32[120,128]{1,0:T(8,128)S(1)}, f32[120,128]{1,0:T(8,128)S(1)}, u32[]{:S(2)}, u32[]{:S(2)}) collective-permute-start(f32[120,128]{1,0:T(8,128)S(1)} %get-tuple-element.19.own_parts), channel_id=1, source_target_pairs={{0,16},{8,24},{16,0},{24,8},{1,17},{9,25},{17,1},{25,9},{2,18},{10... | collective-permute-start | bytes 184328 | tf_op jit(solution)/shard_map/ppermute | solution.py:536
  6.8 5.6 %collective-permute-start.1 = (f32[120,128]{1,0:T(8,128)S(1)}, f32[120,128]{1,0:T(8,128)S(1)}, u32[]{:S(2)}, u32[]{:S(2)}) collective-permute-start(f32[120,128]{1,0:T(8,128)S(1)} %get-tuple-element.19.own_parts), channel_id=1, source_target_pairs={{0,24},{8,16},{16,8},{24,0},{1,25},{9,17},{17,9},{25,1},{2,26},{10... | collective-permute-start | bytes 184328 | tf_op jit(solution)/shard_map/ppermute | solution.py:536
  8.2 4.2 %collective-permute-start.2 = (f32[120,128]{1,0:T(8,128)S(1)}, f32[120,128]{1,0:T(8,128)S(1)}, u32[]{:S(2)}, u32[]{:S(2)}) collective-permute-start(f32[120,128]{1,0:T(8,128)S(1)} %get-tuple-element.19.own_parts), channel_id=1, source_target_pairs={{0,8},{8,0},{16,24},{24,16},{1,9},{9,1},{17,25},{25,17},{2,10},{10... | collective-permute-start | bytes 184328 | tf_op jit(solution)/shard_map/ppermute | solution.py:536
  12.7 4.3 %collective-permute-start.3 = (f32[8,2048]{1,0:T(8,128)S(1)}, f32[8,2048]{1,0:T(8,128)S(1)}, u32[]{:S(2)}, u32[]{:S(2)}) collective-permute-start(f32[8,2048]{1,0:T(8,128)S(1)} %solve.1.refs_0_), channel_id=1, source_target_pairs={{0,1},{1,0},{2,3},{3,2},{4,5},{5,4},{6,7},{7,6},{8,9},{9,8},{10,11... | collective-permute-start | bytes 196616 | tf_op jit(solution)/shard_map/ppermute | solution.py:557
  19.4 4.2 %collective-permute-start.6 = (f32[448,1024]{1,0:T(8,128)S(1)}, f32[448,1024]{1,0:T(8,128)S(1)}, u32[]{:S(2)}, u32[]{:S(2)}) collective-permute-start(f32[448,1024]{1,0:T(8,128)S(1)} %get-tuple-element.33), channel_id=1, source_target_pairs={{0,4},{4,0},{1,5},{5,1},{2,6},{6,2},{3,7},{7,3},{8,12},{12,8},{9,1... | collective-permute-start | bytes 5505032 | tf_op jit(solution)/shard_map/ppermute | solution.py:573
  19.4 4.1 %collective-permute-start.4 = (f32[16,1024]{1,0:T(8,128)S(1)}, f32[16,1024]{1,0:T(8,128)S(1)}, u32[]{:S(2)}, u32[]{:S(2)}) collective-permute-start(f32[16,1024]{1,0:T(8,128)S(1)} %get-tuple-element.30.refs_7_), channel_id=1, source_target_pairs={{0,4},{4,0},{1,5},{5,1},{2,6},{6,2},{3,7},{7,3},{8,12},{12,8},{9,1... | collective-permute-start | bytes 196616 | tf_op jit(solution)/shard_map/ppermute | solution.py:571
  19.9 3.6 %collective-permute-start.5 = (f32[64,128]{1,0:T(8,128)S(1)}, f32[64,128]{1,0:T(8,128)S(1)}, u32[]{:S(2)}, u32[]{:S(2)}) collective-permute-start(f32[64,128]{1,0:T(8,128)S(1)} %get-tuple-element.32), channel_id=1, source_target_pairs={{0,4},{4,0},{1,5},{5,1},{2,6},{6,2},{3,7},{7,3},{8,12},{12,8},{9,1... | collective-permute-start | bytes 98312 | tf_op jit(solution)/shard_map/ppermute | solution.py:572

commit v6 on v5

--- a/solution.py
+++ b/solution.py
@@ -272,7 +272,7 @@
         in_specs=[vmem] * 4,
         out_specs=vmem,
         out_shape=jax.ShapeDtypeStruct((ROWS, groups * LANES), F32),
-        scratch_shapes=[pltpu.VMEM((groups * ROWS, LANES), F32)],
+        scratch_shapes=[pltpu.VMEM((groups * ROWS + ROWS, LANES), F32)],
         compiler_params=pltpu.CompilerParams(vmem_limit_bytes=VMEM_LIMIT),
         name="solve",
     )(*parts)
@@ -482,7 +482,9 @@
             for block in blocks:
                 value = value + block[k * own : (k + 1) * own, tile]
             ready[t, pl.ds(k, own, stride=types), :] = value * scale
-        copy = pltpu.make_async_copy(ready.at[t], out.at[:, pl.ds(t * LANES, LANES)], sems.at[t])
+        copy = pltpu.make_async_copy(
+            ready.at[t, pl.ds(0, types * own)], out.at[:, pl.ds(t * LANES, LANES)], sems.at[t]
+        )
         copy.start()
         copies.append(copy)
 
@@ -521,7 +523,7 @@
             pltpu.VMEM((rows, step), BF16),
             pltpu.VMEM((48, rows), F32),
             pltpu.VMEM((rows, genes - columns), F32),
-            pltpu.VMEM((genes // LANES, types * own, LANES), F32),
+            pltpu.VMEM((genes // LANES, types * own + ROWS, LANES), F32),
             pltpu.SemaphoreType.DMA((genes // LANES,)),
             pltpu.VMEM((halves, types, p[0].shape[1]), F32),
             pltpu.SemaphoreType.DMA((halves,)),

time: 25.8 us -> 25.8 us (level)
  no operation moved by 1% of the time
where the time goes in v6:
time: 25.8 us; the launch traced here: 25.7 us
  Pallas kernels  16.5 us (64%)
  starting transfers between devices  6.86 us (27%)
  waiting for transfers between devices  1.56 us (6%)
  between operations  0.71 us (3%)
    pallas_call x2, Pallas kernels, others_products(): pl.pallas_call(functools.partial(others_kernel, types, step, first_col, b...  4.69 us
    ppermute x3, starting transfers between devices, swap(): return lax.ppermute(part, 'gene', [(i, i ^ offset) for i in range(n_gene)])  4.57 us
    pallas_call x1, Pallas kernels, own_products(): pl.pallas_call(functools.partial(own_kernel, types, step, halves), in_spe...  3.5 us
    pallas_call x1, Pallas kernels, right_sides(): pl.pallas_call(functools.partial(rhs_kernel, types, halves, pieces), in_s...  3.12 us
    pallas_call x1, Pallas kernels, prepare(): pl.pallas_call(functools.partial(prepare_kernel, own, halves, pieces), in...  2.88 us
    pallas_call x1, Pallas kernels, finish(): pl.pallas_call(functools.partial(finish_kernel, types, step, scale, own,...  2.1 us
    ppermute x1, starting transfers between devices, local(): solved.append(lax.ppermute(solved[0], 'variant', pairs))  1.64 us
    ppermute x3, waiting for transfers between devices, swap(): return lax.ppermute(part, 'gene', [(i, i ^ offset) for i in range(n_gene)])  1.21 us
  transfers between devices with their start and end apart: 7, of which 3 were waited for; matrix products, arithmetic and copies ran while one was open for 0% of the time, Pallas kernels for 34%

profile of v6, /device:TPU:0, one launch (start us, length us, event | category | flops | bytes accessed | tf_op | source)
XLA Modules:
  0.0 25.7 jit_solution(8562540775090723618)
XLA Ops:
  0.6 3.1 %right_sides.1 = (bf16[2048,1024]{1,0:T(8,128)(2,1)S(1)}, f32[120,128]{1,0:T(8,128)S(1)}) custom-call(s32[500]{0:T(512)} %signature_in.1, f32[7,1024]{1,0:T(8,128)} %bitcast.2, bf16[4096,1024]{1,0:T(8,128)(2,1)} %expression.3), custom_call_target="tpu_custom_call" | custom-call | flops 134217728 | bytes 4194304 | tf_op jit(solution)/shard_map/right_sides/pallas_call | solution.py:169
  3.8 3.0 %collective-permute-start = (f32[120,128]{1,0:T(8,128)S(1)}, f32[120,128]{1,0:T(8,128)S(1)}, u32[]{:S(2)}, u32[]{:S(2)}) collective-permute-start(f32[120,128]{1,0:T(8,128)S(1)} %get-tuple-element.19.own_parts), channel_id=1, source_target_pairs={{0,16},{8,24},{16,0},{24,8},{1,17},{9,25},{17,1},{25,9},{2,18},{10... | collective-permute-start | bytes 184328 | tf_op jit(solution)/shard_map/ppermute | solution.py:538
  6.8 1.4 %collective-permute-start.1 = (f32[120,128]{1,0:T(8,128)S(1)}, f32[120,128]{1,0:T(8,128)S(1)}, u32[]{:S(2)}, u32[]{:S(2)}) collective-permute-start(f32[120,128]{1,0:T(8,128)S(1)} %get-tuple-element.19.own_parts), channel_id=1, source_target_pairs={{0,24},{8,16},{16,8},{24,0},{1,25},{9,17},{17,9},{25,1},{2,26},{10... | collective-permute-start | bytes 184328 | tf_op jit(solution)/shard_map/ppermute | solution.py:538
  8.2 0.1 collective-permute-start.2
  8.3 2.9 %prepare.1 = (bf16[64,4096]{1,0:T(8,128)(2,1)S(1)}, bf16[64,4096]{1,0:T(8,128)(2,1)S(1)}, bf16[2048,1024]{1,0:T(8,128)(2,1)S(1)}) custom-call(s32[4096,128]{1,0:T(8,128)} %dosage_in.1, bf16[4096,1024]{1,0:T(8,128)(2,1)} %expression.3), custom_call_target="tpu_custom_call" | custom-call | flops 524288 | bytes 3145728 | tf_op jit(solution)/shard_map/prepare/pallas_call | solution.py:228
  11.2 0.0 collective-permute-done.x_parts
  11.2 1.1 %collective-permute-done.1.y_parts = f32[120,128]{1,0:T(8,128)S(1)} collective-permute-done((f32[120,128]{1,0:T(8,128)S(1)}, f32[120,128]{1,0:T(8,128)S(1)}, u32[]{:S(2)}, u32[]{:S(2)}) %collective-permute-start.1) | collective-permute-done | bytes 61472 | tf_op jit(solution)/shard_map/ppermute | solution.py:538
  12.4 0.1 collective-permute-done.2.d_parts
  12.4 0.2 solve.1.refs_0_
  12.7 1.6 %collective-permute-start.3 = (f32[8,2048]{1,0:T(8,128)S(1)}, f32[8,2048]{1,0:T(8,128)S(1)}, u32[]{:S(2)}, u32[]{:S(2)}) collective-permute-start(f32[8,2048]{1,0:T(8,128)S(1)} %solve.1.refs_0_), channel_id=1, source_target_pairs={{0,1},{1,0},{2,3},{3,2},{4,5},{5,4},{6,7},{7,6},{8,9},{9,8},{10,11... | collective-permute-start | bytes 196616 | tf_op jit(solution)/shard_map/ppermute | solution.py:559
  14.3 2.3 %others_products.2 = (f32[448,1024]{1,0:T(8,128)S(1)}, f32[16,1024]{1,0:T(8,128)S(1)}, f32[64,128]{1,0:T(8,128)S(1)}, f32[64,128]{1,0:T(8,128)S(1)}) custom-call(f32[8,2048]{1,0:T(8,128)S(1)} %solve.1.refs_0_, bf16[64,4096]{1,0:T(8,128)(2,1)S(1)} %get-tuple-element.22.refs_4_.refs_1_, bf16[64,4096]{1,0:T(8,128)(2,1)S(1)} %get-tuple-element.25.refs_2_, ...), custom_call_target="tpu_custom_call" | custom-call | flops 1879048192 | bytes 4194304 | tf_op jit(solution)/shard_map/others_products/pallas_call | solution.py:346
  16.7 0.3 %collective-permute-done.3.refs_1_.refs_0_ = f32[8,2048]{1,0:T(8,128)S(1)} collective-permute-done((f32[8,2048]{1,0:T(8,128)S(1)}, f32[8,2048]{1,0:T(8,128)S(1)}, u32[]{:S(2)}, u32[]{:S(2)}) %collective-permute-start.3) | collective-permute-done | bytes 65568 | tf_op jit(solution)/shard_map/ppermute | solution.py:559
  17.0 2.3 %others_products.3 = (f32[448,1024]{1,0:T(8,128)S(1)}, f32[16,1024]{1,0:T(8,128)S(1)}, f32[64,128]{1,0:T(8,128)S(1)}, f32[64,128]{1,0:T(8,128)S(1)}) custom-call(f32[8,2048]{1,0:T(8,128)S(1)} %collective-permute-done.3.refs_1_.refs_0_, bf16[64,4096]{1,0:T(8,128)(2,1)S(1)} %get-tuple-element.22.refs_4_.refs_1_, ...), custom_call_target="tpu_custom_call" | custom-call | flops 1879048192 | bytes 4194304 | tf_op jit(solution)/shard_map/others_products/pallas_call | solution.py:346
  19.4 0.1 collective-permute-start.6
  19.4 0.5 %collective-permute-start.4 = (f32[16,1024]{1,0:T(8,128)S(1)}, f32[16,1024]{1,0:T(8,128)S(1)}, u32[]{:S(2)}, u32[]{:S(2)}) collective-permute-start(f32[16,1024]{1,0:T(8,128)S(1)} %get-tuple-element.30.refs_7_), channel_id=1, source_target_pairs={{0,4},{4,0},{1,5},{5,1},{2,6},{6,2},{3,7},{7,3},{8,12},{12,8},{9,1... | collective-permute-start | bytes 196616 | tf_op jit(solution)/shard_map/ppermute | solution.py:573
  19.9 0.1 collective-permute-start.5
  20.0 3.5 %own_products.1 = (f32[448,768]{1,0:T(8,128)S(1)}, f32[448,256]{1,0:T(8,128)S(1)}) custom-call(f32[8,2048]{1,0:T(8,128)S(1)} %solve.1.refs_0_, f32[8,2048]{1,0:T(8,128)S(1)} %collective-permute-done.3.refs_1_.refs_0_, bf16[2048,1024]{1,0:T(8,128)(2,1)S(1)} %get-tuple-element.20.refs_2_.refs_3_, bf16[2048,1024]{1,0:T(8,128)(2,1)S(1)} %get-tuple-element.21.refs_3_, ...), custom_call_target="tpu_custom_call" | custom-call | flops 2818572288 | bytes 6291456 | tf_op jit(solution)/shard_map/own_products/pallas_call | solution.py:408
  23.5 0.0 collective-permute-done.5.refs_10_
  23.5 0.0 collective-permute-done.4.refs_8_
  23.6 0.0 collective-permute-done.6.refs_11_
  23.6 2.1 %finish.1 = (f32[448,1024]{1,0:T(8,128)}, f32[7,4096]{1,0:T(8,128)}) custom-call(f32[8,2048]{1,0:T(8,128)S(1)} %solve.1.refs_0_, f32[8,2048]{1,0:T(8,128)S(1)} %collective-permute-done.3.refs_1_.refs_0_, bf16[2048,1024]{1,0:T(8,128)(2,1)S(1)} %get-tuple-element.20.refs_2_.refs_3_, bf16[2048,1024]{1,0:T(8,128)(2,1)S(1)} %get-tuple-element.21.refs_3_, ...), custom_call_target="tpu_custom_call" | custom-call | tf_op jit(solution)/shard_map/finish/pallas_call | solution.py:514
Async XLA Ops:
  3.8 7.5 %collective-permute-start = (f32[120,128]{1,0:T(8,128)S(1)}, f32[120,128]{1,0:T(8,128)S(1)}, u32[]{:S(2)}, u32[]{:S(2)}) collective-permute-start(f32[120,128]{1,0:T(8,128)S(1)} %get-tuple-element.19.own_parts), channel_id=1, source_target_pairs={{0,16},{8,24},{16,0},{24,8},{1,17},{9,25},{17,1},{25,9},{2,18},{10... | collective-permute-start | bytes 184328 | tf_op jit(solution)/shard_map/ppermute | solution.py:538
  6.8 5.6 %collective-permute-start.1 = (f32[120,128]{1,0:T(8,128)S(1)}, f32[120,128]{1,0:T(8,128)S(1)}, u32[]{:S(2)}, u32[]{:S(2)}) collective-permute-start(f32[120,128]{1,0:T(8,128)S(1)} %get-tuple-element.19.own_parts), channel_id=1, source_target_pairs={{0,24},{8,16},{16,8},{24,0},{1,25},{9,17},{17,9},{25,1},{2,26},{10... | collective-permute-start | bytes 184328 | tf_op jit(solution)/shard_map/ppermute | solution.py:538
  8.2 4.2 %collective-permute-start.2 = (f32[120,128]{1,0:T(8,128)S(1)}, f32[120,128]{1,0:T(8,128)S(1)}, u32[]{:S(2)}, u32[]{:S(2)}) collective-permute-start(f32[120,128]{1,0:T(8,128)S(1)} %get-tuple-element.19.own_parts), channel_id=1, source_target_pairs={{0,8},{8,0},{16,24},{24,16},{1,9},{9,1},{17,25},{25,17},{2,10},{10... | collective-permute-start | bytes 184328 | tf_op jit(solution)/shard_map/ppermute | solution.py:538
  12.7 4.3 %collective-permute-start.3 = (f32[8,2048]{1,0:T(8,128)S(1)}, f32[8,2048]{1,0:T(8,128)S(1)}, u32[]{:S(2)}, u32[]{:S(2)}) collective-permute-start(f32[8,2048]{1,0:T(8,128)S(1)} %solve.1.refs_0_), channel_id=1, source_target_pairs={{0,1},{1,0},{2,3},{3,2},{4,5},{5,4},{6,7},{7,6},{8,9},{9,8},{10,11... | collective-permute-start | bytes 196616 | tf_op jit(solution)/shard_map/ppermute | solution.py:559
  19.4 4.2 %collective-permute-start.6 = (f32[448,1024]{1,0:T(8,128)S(1)}, f32[448,1024]{1,0:T(8,128)S(1)}, u32[]{:S(2)}, u32[]{:S(2)}) collective-permute-start(f32[448,1024]{1,0:T(8,128)S(1)} %get-tuple-element.33), channel_id=1, source_target_pairs={{0,4},{4,0},{1,5},{5,1},{2,6},{6,2},{3,7},{7,3},{8,12},{12,8},{9,1... | collective-permute-start | bytes 5505032 | tf_op jit(solution)/shard_map/ppermute | solution.py:575
  19.4 4.1 %collective-permute-start.4 = (f32[16,1024]{1,0:T(8,128)S(1)}, f32[16,1024]{1,0:T(8,128)S(1)}, u32[]{:S(2)}, u32[]{:S(2)}) collective-permute-start(f32[16,1024]{1,0:T(8,128)S(1)} %get-tuple-element.30.refs_7_), channel_id=1, source_target_pairs={{0,4},{4,0},{1,5},{5,1},{2,6},{6,2},{3,7},{7,3},{8,12},{12,8},{9,1... | collective-permute-start | bytes 196616 | tf_op jit(solution)/shard_map/ppermute | solution.py:573
  19.9 3.6 %collective-permute-start.5 = (f32[64,128]{1,0:T(8,128)S(1)}, f32[64,128]{1,0:T(8,128)S(1)}, u32[]{:S(2)}, u32[]{:S(2)}) collective-permute-start(f32[64,128]{1,0:T(8,128)S(1)} %get-tuple-element.32), channel_id=1, source_target_pairs={{0,4},{4,0},{1,5},{5,1},{2,6},{6,2},{3,7},{7,3},{8,12},{12,8},{9,1... | collective-permute-start | bytes 98312 | tf_op jit(solution)/shard_map/ppermute | solution.py:574

commit v7 on v6

--- a/solution.py
+++ b/solution.py
@@ -402,7 +402,7 @@
 def own_products(p, mine, held, columns, types):
     halves = len(p)
     samples, genes = halves * p[0].shape[1], held[0].shape[1]
-    step = 512
+    step = 1024
     rows = types * mine.shape[0]
     vmem = pl.BlockSpec(memory_space=pltpu.VMEM)
     return pl.pallas_call(

time: 25.8 us -> 25.8 us (level)
  no operation moved by 1% of the time
where the time goes in v7:
time: 25.8 us; the launch traced here: 25.6 us
  Pallas kernels  16.5 us (64%)
  starting transfers between devices  6.86 us (27%)
  waiting for transfers between devices  1.56 us (6%)
  between operations  0.71 us (3%)
    pallas_call x2, Pallas kernels, others_products(): pl.pallas_call(functools.partial(others_kernel, types, step, first_col, b...  4.69 us
    ppermute x3, starting transfers between devices, swap(): return lax.ppermute(part, 'gene', [(i, i ^ offset) for i in range(n_gene)])  4.57 us
    pallas_call x1, Pallas kernels, own_products(): pl.pallas_call(functools.partial(own_kernel, types, step, halves), in_spe...  3.47 us
    pallas_call x1, Pallas kernels, right_sides(): pl.pallas_call(functools.partial(rhs_kernel, types, halves, pieces), in_s...  3.12 us
    pallas_call x1, Pallas kernels, prepare(): pl.pallas_call(functools.partial(prepare_kernel, own, halves, pieces), in...  2.88 us
    pallas_call x1, Pallas kernels, finish(): pl.pallas_call(functools.partial(finish_kernel, types, step, scale, own,...  2.1 us
    ppermute x1, starting transfers between devices, local(): solved.append(lax.ppermute(solved[0], 'variant', pairs))  1.64 us
    ppermute x3, waiting for transfers between devices, swap(): return lax.ppermute(part, 'gene', [(i, i ^ offset) for i in range(n_gene)])  1.21 us
  transfers between devices with their start and end apart: 7, of which 3 were waited for; matrix products, arithmetic and copies ran while one was open for 0% of the time, Pallas kernels for 34%

profile of v7, /device:TPU:0, one launch (start us, length us, event | category | flops | bytes accessed | tf_op | source)
XLA Modules:
  0.0 25.6 jit_solution(9613331580851620725)
XLA Ops:
  0.6 3.1 %right_sides.1 = (bf16[2048,1024]{1,0:T(8,128)(2,1)S(1)}, f32[120,128]{1,0:T(8,128)S(1)}) custom-call(s32[500]{0:T(512)} %signature_in.1, f32[7,1024]{1,0:T(8,128)} %bitcast.2, bf16[4096,1024]{1,0:T(8,128)(2,1)} %expression.3), custom_call_target="tpu_custom_call" | custom-call | flops 134217728 | bytes 4194304 | tf_op jit(solution)/shard_map/right_sides/pallas_call | solution.py:169
  3.8 3.0 %collective-permute-start = (f32[120,128]{1,0:T(8,128)S(1)}, f32[120,128]{1,0:T(8,128)S(1)}, u32[]{:S(2)}, u32[]{:S(2)}) collective-permute-start(f32[120,128]{1,0:T(8,128)S(1)} %get-tuple-element.19.own_parts), channel_id=1, source_target_pairs={{0,16},{8,24},{16,0},{24,8},{1,17},{9,25},{17,1},{25,9},{2,18},{10... | collective-permute-start | bytes 184328 | tf_op jit(solution)/shard_map/ppermute | solution.py:538
  6.8 1.4 %collective-permute-start.1 = (f32[120,128]{1,0:T(8,128)S(1)}, f32[120,128]{1,0:T(8,128)S(1)}, u32[]{:S(2)}, u32[]{:S(2)}) collective-permute-start(f32[120,128]{1,0:T(8,128)S(1)} %get-tuple-element.19.own_parts), channel_id=1, source_target_pairs={{0,24},{8,16},{16,8},{24,0},{1,25},{9,17},{17,9},{25,1},{2,26},{10... | collective-permute-start | bytes 184328 | tf_op jit(solution)/shard_map/ppermute | solution.py:538
  8.2 0.1 collective-permute-start.2
  8.3 2.9 %prepare.1 = (bf16[64,4096]{1,0:T(8,128)(2,1)S(1)}, bf16[64,4096]{1,0:T(8,128)(2,1)S(1)}, bf16[2048,1024]{1,0:T(8,128)(2,1)S(1)}) custom-call(s32[4096,128]{1,0:T(8,128)} %dosage_in.1, bf16[4096,1024]{1,0:T(8,128)(2,1)} %expression.3), custom_call_target="tpu_custom_call" | custom-call | flops 524288 | bytes 3145728 | tf_op jit(solution)/shard_map/prepare/pallas_call | solution.py:228
  11.2 0.0 collective-permute-done.x_parts
  11.2 1.1 %collective-permute-done.1.y_parts = f32[120,128]{1,0:T(8,128)S(1)} collective-permute-done((f32[120,128]{1,0:T(8,128)S(1)}, f32[120,128]{1,0:T(8,128)S(1)}, u32[]{:S(2)}, u32[]{:S(2)}) %collective-permute-start.1) | collective-permute-done | bytes 61472 | tf_op jit(solution)/shard_map/ppermute | solution.py:538
  12.4 0.1 collective-permute-done.2.d_parts
  12.4 0.2 solve.1.refs_0_
  12.7 1.6 %collective-permute-start.3 = (f32[8,2048]{1,0:T(8,128)S(1)}, f32[8,2048]{1,0:T(8,128)S(1)}, u32[]{:S(2)}, u32[]{:S(2)}) collective-permute-start(f32[8,2048]{1,0:T(8,128)S(1)} %solve.1.refs_0_), channel_id=1, source_target_pairs={{0,1},{1,0},{2,3},{3,2},{4,5},{5,4},{6,7},{7,6},{8,9},{9,8},{10,11... | collective-permute-start | bytes 196616 | tf_op jit(solution)/shard_map/ppermute | solution.py:559
  14.3 2.3 %others_products.2 = (f32[448,1024]{1,0:T(8,128)S(1)}, f32[16,1024]{1,0:T(8,128)S(1)}, f32[64,128]{1,0:T(8,128)S(1)}, f32[64,128]{1,0:T(8,128)S(1)}) custom-call(f32[8,2048]{1,0:T(8,128)S(1)} %solve.1.refs_0_, bf16[64,4096]{1,0:T(8,128)(2,1)S(1)} %get-tuple-element.22.refs_4_.refs_1_, bf16[64,4096]{1,0:T(8,128)(2,1)S(1)} %get-tuple-element.25.refs_2_, ...), custom_call_target="tpu_custom_call" | custom-call | flops 1879048192 | bytes 4194304 | tf_op jit(solution)/shard_map/others_products/pallas_call | solution.py:346
  16.7 0.3 %collective-permute-done.3.refs_1_.refs_0_ = f32[8,2048]{1,0:T(8,128)S(1)} collective-permute-done((f32[8,2048]{1,0:T(8,128)S(1)}, f32[8,2048]{1,0:T(8,128)S(1)}, u32[]{:S(2)}, u32[]{:S(2)}) %collective-permute-start.3) | collective-permute-done | bytes 65568 | tf_op jit(solution)/shard_map/ppermute | solution.py:559
  17.0 2.3 %others_products.3 = (f32[448,1024]{1,0:T(8,128)S(1)}, f32[16,1024]{1,0:T(8,128)S(1)}, f32[64,128]{1,0:T(8,128)S(1)}, f32[64,128]{1,0:T(8,128)S(1)}) custom-call(f32[8,2048]{1,0:T(8,128)S(1)} %collective-permute-done.3.refs_1_.refs_0_, bf16[64,4096]{1,0:T(8,128)(2,1)S(1)} %get-tuple-element.22.refs_4_.refs_1_, ...), custom_call_target="tpu_custom_call" | custom-call | flops 1879048192 | bytes 4194304 | tf_op jit(solution)/shard_map/others_products/pallas_call | solution.py:346
  19.4 0.1 collective-permute-start.6
  19.4 0.5 %collective-permute-start.4 = (f32[16,1024]{1,0:T(8,128)S(1)}, f32[16,1024]{1,0:T(8,128)S(1)}, u32[]{:S(2)}, u32[]{:S(2)}) collective-permute-start(f32[16,1024]{1,0:T(8,128)S(1)} %get-tuple-element.30.refs_7_), channel_id=1, source_target_pairs={{0,4},{4,0},{1,5},{5,1},{2,6},{6,2},{3,7},{7,3},{8,12},{12,8},{9,1... | collective-permute-start | bytes 196616 | tf_op jit(solution)/shard_map/ppermute | solution.py:573
  19.9 0.1 collective-permute-start.5
  20.0 3.5 %own_products.1 = (f32[448,768]{1,0:T(8,128)S(1)}, f32[448,256]{1,0:T(8,128)S(1)}) custom-call(f32[8,2048]{1,0:T(8,128)S(1)} %solve.1.refs_0_, f32[8,2048]{1,0:T(8,128)S(1)} %collective-permute-done.3.refs_1_.refs_0_, bf16[2048,1024]{1,0:T(8,128)(2,1)S(1)} %get-tuple-element.20.refs_2_.refs_3_, bf16[2048,1024]{1,0:T(8,128)(2,1)S(1)} %get-tuple-element.21.refs_3_, ...), custom_call_target="tpu_custom_call" | custom-call | flops 2818572288 | bytes 6291456 | tf_op jit(solution)/shard_map/own_products/pallas_call | solution.py:408
  23.5 0.0 collective-permute-done.5.refs_10_
  23.5 0.0 collective-permute-done.4.refs_8_
  23.5 0.0 collective-permute-done.6.refs_11_
  23.5 2.1 %finish.1 = (f32[448,1024]{1,0:T(8,128)}, f32[7,4096]{1,0:T(8,128)}) custom-call(f32[8,2048]{1,0:T(8,128)S(1)} %solve.1.refs_0_, f32[8,2048]{1,0:T(8,128)S(1)} %collective-permute-done.3.refs_1_.refs_0_, bf16[2048,1024]{1,0:T(8,128)(2,1)S(1)} %get-tuple-element.20.refs_2_.refs_3_, bf16[2048,1024]{1,0:T(8,128)(2,1)S(1)} %get-tuple-element.21.refs_3_, ...), custom_call_target="tpu_custom_call" | custom-call | tf_op jit(solution)/shard_map/finish/pallas_call | solution.py:514
Async XLA Ops:
  3.8 7.5 %collective-permute-start = (f32[120,128]{1,0:T(8,128)S(1)}, f32[120,128]{1,0:T(8,128)S(1)}, u32[]{:S(2)}, u32[]{:S(2)}) collective-permute-start(f32[120,128]{1,0:T(8,128)S(1)} %get-tuple-element.19.own_parts), channel_id=1, source_target_pairs={{0,16},{8,24},{16,0},{24,8},{1,17},{9,25},{17,1},{25,9},{2,18},{10... | collective-permute-start | bytes 184328 | tf_op jit(solution)/shard_map/ppermute | solution.py:538
  6.8 5.6 %collective-permute-start.1 = (f32[120,128]{1,0:T(8,128)S(1)}, f32[120,128]{1,0:T(8,128)S(1)}, u32[]{:S(2)}, u32[]{:S(2)}) collective-permute-start(f32[120,128]{1,0:T(8,128)S(1)} %get-tuple-element.19.own_parts), channel_id=1, source_target_pairs={{0,24},{8,16},{16,8},{24,0},{1,25},{9,17},{17,9},{25,1},{2,26},{10... | collective-permute-start | bytes 184328 | tf_op jit(solution)/shard_map/ppermute | solution.py:538
  8.2 4.2 %collective-permute-start.2 = (f32[120,128]{1,0:T(8,128)S(1)}, f32[120,128]{1,0:T(8,128)S(1)}, u32[]{:S(2)}, u32[]{:S(2)}) collective-permute-start(f32[120,128]{1,0:T(8,128)S(1)} %get-tuple-element.19.own_parts), channel_id=1, source_target_pairs={{0,8},{8,0},{16,24},{24,16},{1,9},{9,1},{17,25},{25,17},{2,10},{10... | collective-permute-start | bytes 184328 | tf_op jit(solution)/shard_map/ppermute | solution.py:538
  12.7 4.3 %collective-permute-start.3 = (f32[8,2048]{1,0:T(8,128)S(1)}, f32[8,2048]{1,0:T(8,128)S(1)}, u32[]{:S(2)}, u32[]{:S(2)}) collective-permute-start(f32[8,2048]{1,0:T(8,128)S(1)} %solve.1.refs_0_), channel_id=1, source_target_pairs={{0,1},{1,0},{2,3},{3,2},{4,5},{5,4},{6,7},{7,6},{8,9},{9,8},{10,11... | collective-permute-start | bytes 196616 | tf_op jit(solution)/shard_map/ppermute | solution.py:559
  19.4 4.2 %collective-permute-start.6 = (f32[448,1024]{1,0:T(8,128)S(1)}, f32[448,1024]{1,0:T(8,128)S(1)}, u32[]{:S(2)}, u32[]{:S(2)}) collective-permute-start(f32[448,1024]{1,0:T(8,128)S(1)} %get-tuple-element.33), channel_id=1, source_target_pairs={{0,4},{4,0},{1,5},{5,1},{2,6},{6,2},{3,7},{7,3},{8,12},{12,8},{9,1... | collective-permute-start | bytes 5505032 | tf_op jit(solution)/shard_map/ppermute | solution.py:575
  19.4 4.1 %collective-permute-start.4 = (f32[16,1024]{1,0:T(8,128)S(1)}, f32[16,1024]{1,0:T(8,128)S(1)}, u32[]{:S(2)}, u32[]{:S(2)}) collective-permute-start(f32[16,1024]{1,0:T(8,128)S(1)} %get-tuple-element.30.refs_7_), channel_id=1, source_target_pairs={{0,4},{4,0},{1,5},{5,1},{2,6},{6,2},{3,7},{7,3},{8,12},{12,8},{9,1... | collective-permute-start | bytes 196616 | tf_op jit(solution)/shard_map/ppermute | solution.py:573
  19.9 3.6 %collective-permute-start.5 = (f32[64,128]{1,0:T(8,128)S(1)}, f32[64,128]{1,0:T(8,128)S(1)}, u32[]{:S(2)}, u32[]{:S(2)}) collective-permute-start(f32[64,128]{1,0:T(8,128)S(1)} %get-tuple-element.32), channel_id=1, source_target_pairs={{0,4},{4,0},{1,5},{5,1},{2,6},{6,2},{3,7},{7,3},{8,12},{12,8},{9,1... | collective-permute-start | bytes 98312 | tf_op jit(solution)/shard_map/ppermute | solution.py:574
